TPU v7x, 32 devices: a whole 2x2x4 slice. The times are simulated.
32 devices in a mesh: row: 4 (over y, x), col: 8 (over z, core).
Axes of the slice: x: 2, y: 2, z: 4, core: 2. Of those that a mesh axis runs over, the one named last changes fastest.
Arguments:
- images: bfloat16 [704, 1152], P(('row', 'col')), may hold values from -0.1875 to 0.1875
- texts: bfloat16 [704, 1152], P(('col', 'row')), may hold values from -0.1875 to 0.1875
- logarithmic_scale: float32 [], replicated, may hold values from 2 to 3
- similarity_bias: float32 [], replicated, may hold values from -4 to -1
Outputs:
- grad_images: float32 [704, 1152], P(('row', 'col'))
- grad_texts: float32 [704, 1152], P(('col', 'row'))
All inputs are finite; a program needn't handle non-finite values.
Results may differ from a plain program's by a relative error of at most 0.03.
Values may be sent and summed in bfloat16 or wider, within the bound.
A program may use at most 64 MiB of HBM per device.

v0:
```python
import jax
import jax.numpy as jnp
from jax import lax
from jax.sharding import PartitionSpec as P


def normalize(values):
    wide = values.astype(jnp.float32)
    length = jnp.sqrt(jnp.sum(wide * wide, axis=1, keepdims=True) + 1e-06)
    return (wide / length, length)


def norm_back(normed, length, upstream):
    along = jnp.sum(normed * upstream, axis=1, keepdims=True)
    return (upstream - normed * along) / length


def pairwise_factors(
    selected_entries, row_offset, column_ranges, column_offset, logit_multiplier, similarity_bias
):
    similarity_logits = lax.dot_general(
        selected_entries,
        column_ranges,
        (((1,), (1,)), ((), ())),
        preferred_element_type=jnp.float32,
    )
    row_ids = row_offset + lax.broadcasted_iota(jnp.int32, similarity_logits.shape, 0)
    col_ids = column_offset + lax.broadcasted_iota(jnp.int32, similarity_logits.shape, 1)
    pair_targets = jnp.where(row_ids == col_ids, jnp.float32(1.0), jnp.float32(-1.0))
    signed_logit = pair_targets * (logit_multiplier * similarity_logits + similarity_bias)
    return (-pair_targets * jax.nn.sigmoid(-signed_logit)).astype(jnp.bfloat16)


def on_device(images, texts, logarithmic_scale, similarity_bias):
    img_unit, img_len = normalize(images)
    txt_unit, txt_len = normalize(texts)
    picture_block = lax.all_gather(img_unit.astype(jnp.bfloat16), "col", axis=0, tiled=True)
    caption_block = lax.all_gather(txt_unit.astype(jnp.bfloat16), "row", axis=0, tiled=True)
    logit_multiplier = jnp.exp(logarithmic_scale)
    row_offset = lax.axis_index("row") * picture_block.shape[0]
    column_offset = lax.axis_index("col") * caption_block.shape[0]
    sigmoid_factors = pairwise_factors(
        picture_block, row_offset, caption_block, column_offset, logit_multiplier, similarity_bias
    )
    caption_contribution = logit_multiplier * lax.dot_general(
        sigmoid_factors, picture_block, (((0,), (0,)), ((), ())), preferred_element_type=jnp.float32
    )
    picture_contribution = logit_multiplier * jnp.dot(
        sigmoid_factors, caption_block, preferred_element_type=jnp.float32
    )
    grad_img_unit = lax.psum_scatter(
        picture_contribution.astype(jnp.bfloat16), "col", scatter_dimension=0, tiled=True
    ).astype(jnp.float32)
    grad_txt_unit = lax.psum_scatter(
        caption_contribution.astype(jnp.bfloat16), "row", scatter_dimension=0, tiled=True
    ).astype(jnp.float32)
    return (
        norm_back(img_unit, img_len, grad_img_unit),
        norm_back(txt_unit, txt_len, grad_txt_unit),
    )


def solution(mesh):
    return jax.shard_map(
        on_device,
        mesh=mesh,
        in_specs=(P(("row", "col"), None), P(("col", "row"), None), P(), P()),
        out_specs=(P(("row", "col"), None), P(("col", "row"), None)),
        check_vma=False,
    )
```

profile of v0, /device:TPU:1, one launch (start us, length us, event | category | flops | bytes accessed | tf_op | source)
XLA Modules:
  0.0 87.6 jit_solution(16405905654121672967)
XLA Ops:
  0.6 1.0 %fusion.11 = f32[22]{0:T(128)S(1)} fusion(bf16[22,1152]{1,0:T(8,128)(2,1)} %param.4), kind=kLoop, calls=%fused_computation.21 | loop fusion | flops 76010 | bytes 50776 | tf_op jit(solution)/shard_map/reduce_sum | solution.py:9
  1.7 16.2 %all-gather = bf16[8,22,1152]{2,1,0:T(8,128)(2,1)S(1)} all-gather(bf16[1,22,1152]{2,1,0:T(8,128)(2,1)S(1)} %convert_bitcast_fusion.1), channel_id=1, replica_groups=mesh['row'=4,'col'=8] {'col'}, dimensions={0}, use_global_device_ids=true | all-gather | bytes 456192 | tf_op jit(solution)/shard_map/all_gather | solution.py:37
  18.0 0.1 reshape.19
  18.1 0.7 copy-done
  18.8 0.1 fusion.12
  18.9 0.1 convert_bitcast_fusion
  19.0 6.8 %all-gather.1 = bf16[4,22,1152]{2,1,0:T(8,128)(2,1)S(1)} all-gather(bf16[1,22,1152]{2,1,0:T(8,128)(2,1)S(1)} %convert_bitcast_fusion), channel_id=1, replica_groups=mesh['row'=4,'col'=8] {'row'}, dimensions={0}, use_global_device_ids=true | all-gather | bytes 253440 | tf_op jit(solution)/shard_map/all_gather | solution.py:38
  27.3 0.3 fusion.10
  27.6 0.2 fusion.3
  27.9 22.5 %fusion.1 = bf16[32,1152]{1,0:T(8,128)(2,1)S(1)} fusion(bf16[88,1152]{1,0:T(8,128)(2,1)S(1)} %fusion.3), kind=kCustom, calls=%all-reduce-scatter.1 | all-reduce-scatter fusion | flops 147457 | bytes 276992
  50.4 2.2 %collective-permute-start.3 = (bf16[30,1152]{1,0:T(8,128)(2,1)S(1)}, bf16[30,1152]{1,0:T(8,128)(2,1)S(1)}, u32[]{:S(2)}, u32[]{:S(2)}) collective-permute-start(bf16[30,1152]{1,0:T(8,128)(2,1)S(1)} %slice.1), channel_id=1, source_target_pairs={{0,8},{8,16},{16,24},{1,9},{9,17},{17,25},{2,10},{10,18},{18,26},{... | collective-permute-start | bytes 207368
  52.6 0.3 fusion.2
  52.9 19.5 %fusion = bf16[32,1152]{1,0:T(8,128)(2,1)S(1)} fusion(bf16[176,1152]{1,0:T(8,128)(2,1)S(1)} %fusion.2), kind=kCustom, calls=%all-reduce-scatter | all-reduce-scatter fusion | flops 294913 | bytes 479744
  72.5 2.9 %collective-permute-start = (bf16[32,1152]{1,0:T(8,128)(2,1)S(1)}, bf16[32,1152]{1,0:T(8,128)(2,1)S(1)}, u32[]{:S(2)}, u32[]{:S(2)}) collective-permute-start(bf16[32,1152]{1,0:T(8,128)(2,1)S(1)} %fusion), channel_id=1, source_target_pairs={{0,1},{1,2},{2,3},{3,4},{4,5},{5,6},{6,7},{8,9},{9,10},{10,11},{11... | collective-permute-start | bytes 221192
  75.3 1.3 %collective-permute-start.1 = (bf16[32,1152]{1,0:T(8,128)(2,1)S(1)}, bf16[32,1152]{1,0:T(8,128)(2,1)S(1)}, u32[]{:S(2)}, u32[]{:S(2)}) collective-permute-start(bf16[32,1152]{1,0:T(8,128)(2,1)S(1)} %fusion), channel_id=1, source_target_pairs={{0,2},{1,3},{2,4},{3,5},{4,6},{5,7},{8,10},{9,11},{10,12},{11,13},... | collective-permute-start | bytes 221192
  76.6 5.4 %collective-permute-start.2 = (bf16[6,1152]{1,0:T(8,128)(2,1)S(1)}, bf16[6,1152]{1,0:T(8,128)(2,1)S(1)}, u32[]{:S(2)}, u32[]{:S(2)}) collective-permute-start(bf16[6,1152]{1,0:T(8,128)(2,1)S(1)} %slice), channel_id=1, source_target_pairs={{0,3},{1,4},{2,5},{3,6},{4,7},{8,11},{9,12},{10,13},{11,14},{12,15... | collective-permute-start | bytes 41480
  82.1 0.6 dynamic-slice.10
  82.8 0.6 dynamic-slice.6
  84.7 0.3 concatenate.1
  85.0 0.2 fusion.15
  85.2 0.7 fusion.16
  85.9 0.7 concatenate
  86.7 0.2 fusion.13
  86.9 0.7 fusion.14
  (19 shorter events, 0.3 us)
Async XLA Ops:
  0.6 1.0 %copy-start.1 = (bf16[22,1152]{1,0:T(8,128)(2,1)S(1)}, bf16[22,1152]{1,0:T(8,128)(2,1)}, u32[]{:S(2)}) copy-start(bf16[22,1152]{1,0:T(8,128)(2,1)} %param.4) | copy-start | bytes 152068
  18.0 0.8 copy-start
  50.4 34.2 %collective-permute-start.3 = (bf16[30,1152]{1,0:T(8,128)(2,1)S(1)}, bf16[30,1152]{1,0:T(8,128)(2,1)S(1)}, u32[]{:S(2)}, u32[]{:S(2)}) collective-permute-start(bf16[30,1152]{1,0:T(8,128)(2,1)S(1)} %slice.1), channel_id=1, source_target_pairs={{0,8},{8,16},{16,24},{1,9},{9,17},{17,25},{2,10},{10,18},{18,26},{... | collective-permute-start | bytes 207368
  72.5 13.5 %collective-permute-start = (bf16[32,1152]{1,0:T(8,128)(2,1)S(1)}, bf16[32,1152]{1,0:T(8,128)(2,1)S(1)}, u32[]{:S(2)}, u32[]{:S(2)}) collective-permute-start(bf16[32,1152]{1,0:T(8,128)(2,1)S(1)} %fusion), channel_id=1, source_target_pairs={{0,1},{1,2},{2,3},{3,4},{4,5},{5,6},{6,7},{8,9},{9,10},{10,11},{11... | collective-permute-start | bytes 221192
  75.3 10.6 %collective-permute-start.1 = (bf16[32,1152]{1,0:T(8,128)(2,1)S(1)}, bf16[32,1152]{1,0:T(8,128)(2,1)S(1)}, u32[]{:S(2)}, u32[]{:S(2)}) collective-permute-start(bf16[32,1152]{1,0:T(8,128)(2,1)S(1)} %fusion), channel_id=1, source_target_pairs={{0,2},{1,3},{2,4},{3,5},{4,6},{5,7},{8,10},{9,11},{10,12},{11,13},... | collective-permute-start | bytes 221192
  76.6 5.5 %copy-start.3 = (u32[32]{0:T(128)S(1)}, u32[32]{0:T(128)}, u32[]{:S(2)}) copy-start(u32[32]{0:T(128)} %constant.29) | copy-start | bytes 388
  76.6 9.3 %collective-permute-start.2 = (bf16[6,1152]{1,0:T(8,128)(2,1)S(1)}, bf16[6,1152]{1,0:T(8,128)(2,1)S(1)}, u32[]{:S(2)}, u32[]{:S(2)}) collective-permute-start(bf16[6,1152]{1,0:T(8,128)(2,1)S(1)} %slice), channel_id=1, source_target_pairs={{0,3},{1,4},{2,5},{3,6},{4,7},{8,11},{9,12},{10,13},{11,14},{12,15... | collective-permute-start | bytes 41480
  82.1 0.7 copy-start.2
where the time goes:
time: 88.1 us; the launch traced here: 87.6 us
  blocking collectives  65.2 us (74%)
  starting transfers between devices  11.8 us (13%)
  between operations  3.47 us (4%)
  local copies, waits for them, and re-layouts  3.2 us (4%)
  other arithmetic  3.2 us (4%)
    unnamed x2, blocking collectives  42.1 us
    all_gather x1, blocking collectives, on_device(): lax.all_gather(img_unit.astype(jnp.bfloat16), 'col', axis=0, tiled=True)  16.2 us
    unnamed x4, starting transfers between devices  11.8 us
    all_gather x1, blocking collectives, on_device(): lax.all_gather(txt_unit.astype(jnp.bfloat16), 'row', axis=0, tiled=True)  6.85 us
    unnamed x16, local copies, waits for them, and re-layouts  3.2 us
  transfers between devices with their start and end apart: 4, of which 0 were waited for; matrix products, arithmetic and copies ran while one was open for 25% of the time, Pallas kernels for 0%

commit v1 on v0

v1 whole, which is shorter than its diff:
```python
import functools

import jax
import jax.numpy as jnp
from jax import lax
from jax.experimental import pallas as pl
from jax.experimental.pallas import tpu as pltpu
from jax.sharding import PartitionSpec as P

MESH = pl.DeviceIdType.MESH
F32, BF16 = jnp.float32, jnp.bfloat16


def unit_rows(x_ref, wide, length_ref, unit_ref):
    rows = x_ref.shape[0]
    wide[...] = jnp.zeros_like(wide)
    wide[:rows] = x_ref[...].astype(F32)
    x = wide[...]
    length = jnp.sqrt(jnp.sum(x * x, axis=1, keepdims=True) + 1e-06)
    unit = x / length
    unit_ref[...] = unit
    length_ref[...] = jnp.broadcast_to(length, length_ref.shape)
    return unit.astype(BF16)


def norm_back(unit, length, upstream):
    along = jnp.sum(unit * upstream, axis=1, keepdims=True)
    return (upstream - unit * along) / length


def kernel(n_row, n_col, cores, img_ref, txt_ref, scale_ref, bias_ref, gimg_ref, gtxt_ref,
           wide, iu, tu, il, tl, gi, gt, wt, pi, pt, ri, rt,
           si, ci, st, ct, si2, ci2, st2, ct2):
    rows = img_ref.shape[0]
    pad = gi.shape[1]
    n_i, n_t = n_row * cores, n_col // cores
    row, col = lax.axis_index("row"), lax.axis_index("col")
    plane, core = col // cores, col % cores
    me_i, me_t = row * cores + core, plane

    def at_i(g):
        return (g // cores, plane * cores + g % cores)

    def at_t(h):
        return (row, h * cores + core)

    to_i = [lax.rem(me_i + k, n_i) for k in range(1, n_i)]
    to_t = [lax.rem(me_t + k, n_t) for k in range(1, n_t)]

    barrier = pltpu.get_barrier_semaphore()
    for h in to_t:
        pl.semaphore_signal(barrier, inc=1, device_id=at_t(h), device_id_type=MESH)
    for g in to_i:
        pl.semaphore_signal(barrier, inc=1, device_id=at_i(g), device_id_type=MESH)
    gt[me_t] = unit_rows(txt_ref, wide, tl, tu)
    gi[me_i] = unit_rows(img_ref, wide, il, iu)
    pl.semaphore_wait(barrier, n_i + n_t - 2)

    def spread(src_of, dst, mine, partners, place, send, recv):
        copies = []
        for k, other in enumerate(partners):
            copy = pltpu.make_async_remote_copy(
                src_ref=src_of(other), dst_ref=dst.at[mine],
                send_sem=send.at[k], recv_sem=recv.at[mine],
                device_id=place(other), device_id_type=MESH)
            copy.start()
            copies.append(copy)
        return copies

    def arrived(dst, other, recv, send):
        pltpu.make_async_remote_copy(
            src_ref=dst.at[other], dst_ref=dst.at[other],
            send_sem=send.at[0], recv_sem=recv.at[other],
            device_id=(row, col), device_id_type=MESH).wait_recv()

    sent = spread(lambda h: gt.at[me_t], gt, me_t, to_t, at_t, st, ct)
    sent += spread(lambda g: gi.at[me_i], gi, me_i, to_i, at_i, si, ci)
    for h in to_t:
        arrived(gt, h, ct, st)
    for g in to_i:
        arrived(gi, g, ci, si)

    images = gi[...].reshape(n_i * pad, -1)
    texts = gt[...].reshape(n_t * pad, -1)
    temperature = jnp.exp(jnp.full((1, 1), scale_ref[0], F32))
    scores = lax.dot_general(images, texts, (((1,), (1,)), ((), ())), preferred_element_type=F32)
    r = lax.broadcasted_iota(jnp.int32, scores.shape, 0)
    c = lax.broadcasted_iota(jnp.int32, scores.shape, 1)
    g, h = r // pad, c // pad
    row_ids = ((g // cores) * n_col + plane * cores + g % cores) * rows + r % pad
    col_ids = ((h * cores + core) * n_row + row) * rows + c % pad
    label = jnp.where(row_ids == col_ids, F32(1.0), F32(-1.0))
    margin = label * (temperature * scores + bias_ref[0])
    weights = -label * jax.nn.sigmoid(-margin)
    wt[...] = weights.T.astype(BF16)
    pt[...] = jnp.dot(wt[...], images, preferred_element_type=F32).astype(BF16).reshape(pt.shape)
    sent += spread(lambda h: pt.at[h], rt, me_t, to_t, at_t, st2, ct2)
    pi[...] = jnp.dot(weights.astype(BF16), texts, preferred_element_type=F32).astype(BF16).reshape(pi.shape)
    sent += spread(lambda g: pi.at[g], ri, me_i, to_i, at_i, si2, ci2)

    total = pt[me_t].astype(F32)
    for h in to_t:
        arrived(rt, h, ct2, st2)
        total += rt[h].astype(F32)
    gtxt_ref[...] = norm_back(tu[...], tl[:, :1], temperature * total)[:rows]
    total = pi[me_i].astype(F32)
    for g in to_i:
        arrived(ri, g, ci2, si2)
        total += ri[g].astype(F32)
    gimg_ref[...] = norm_back(iu[...], il[:, :1], temperature * total)[:rows]
    for copy in sent:
        copy.wait_send()


def on_device(n_row, n_col, images, texts, logarithmic_scale, similarity_bias):
    rows, width = images.shape
    pad = -(-rows // 16) * 16
    cores = 2 if n_col % 2 == 0 else 1
    n_i, n_t = n_row * cores, n_col // cores
    vmem = pl.BlockSpec(memory_space=pltpu.VMEM)
    smem = pl.BlockSpec(memory_space=pltpu.SMEM)
    out = jax.ShapeDtypeStruct((rows, width), F32)
    dma = pltpu.SemaphoreType.DMA
    return pl.pallas_call(
        functools.partial(kernel, n_row, n_col, cores),
        out_shape=(out, out),
        in_specs=[vmem, vmem, smem, smem],
        out_specs=(vmem, vmem),
        scratch_shapes=[
            pltpu.VMEM((pad, width), F32),
            pltpu.VMEM((pad, width), F32),
            pltpu.VMEM((pad, width), F32),
            pltpu.VMEM((pad, 128), F32),
            pltpu.VMEM((pad, 128), F32),
            pltpu.VMEM((n_i, pad, width), BF16),
            pltpu.VMEM((n_t, pad, width), BF16),
            pltpu.VMEM((n_t * pad, n_i * pad), BF16),
            pltpu.VMEM((n_i, pad, width), BF16),
            pltpu.VMEM((n_t, pad, width), BF16),
            pltpu.VMEM((n_i, pad, width), BF16),
            pltpu.VMEM((n_t, pad, width), BF16),
            dma((n_i,)), dma((n_i,)), dma((n_t,)), dma((n_t,)),
            dma((n_i,)), dma((n_i,)), dma((n_t,)), dma((n_t,)),
        ],
        compiler_params=pltpu.CompilerParams(
            collective_id=0, has_side_effects=True, vmem_limit_bytes=48 * 2**20),
    )(images, texts, logarithmic_scale.reshape(1), similarity_bias.reshape(1))


def solution(mesh):
    return jax.shard_map(
        functools.partial(on_device, mesh.shape["row"], mesh.shape["col"]),
        mesh=mesh,
        in_specs=(P(("row", "col"), None), P(("col", "row"), None), P(), P()),
        out_specs=(P(("row", "col"), None), P(("col", "row"), None)),
        check_vma=False,
    )
```

time: 88.1 us -> 27.9 us (0.32)
  blocking collectives: 65.2 us -> 0 us
  Pallas kernels: 0 us -> 22.8 us
  starting transfers between devices: 11.8 us -> 0 us
  other arithmetic: 3.2 us -> 0 us
  between operations: 3.47 us -> 1.94 us
    unnamed x2 -> x0, blocking collectives: 42.1 us -> none
    all_gather x2 -> x0, blocking collectives: 23.1 us -> none  [the longest x1 16.2 us: on_device(): lax.all_gather(img_unit.astype(jnp.bfloat16), 'col', axis=0, tiled=True)]
    pallas_call x0 -> x1, Pallas kernels: none -> 22.8 us  [on_device(): pl.pallas_call(functools.partial(kernel, n_row, n_col, cores), out_shape=...]
    unnamed x4 -> x0, starting transfers between devices: 11.8 us -> none
    reduce_sum x4 -> x0, other arithmetic: 1.52 us -> none  [the longest x2 1.12 us: normalize(): length = jnp.sqrt(jnp.sum(wide * wide, axis=1, keepdims=True) + 1e-06)]
    div x2 -> x0, other arithmetic: 1.49 us -> none  [norm_back(): return (upstream - normed * along) / length]
    unnamed x16 -> x6, local copies, waits for them, and re-layouts: 3.2 us -> 2.91 us
  transfers between devices with their start and end apart: 4 -> 0, of which waited for: 0 -> 0; matrix products, arithmetic and copies ran while one was open for 25% -> 0% of each run, Pallas kernels for 0% -> 0%
where the time goes in v1:
time: 27.9 us; the launch traced here: 27.6 us
  Pallas kernels  22.8 us (82%)
  local copies, waits for them, and re-layouts  2.91 us (10%)
  between operations  1.94 us (7%)
    pallas_call x1, Pallas kernels, on_device(): pl.pallas_call(functools.partial(kernel, n_row, n_col, cores), out_shape=...  22.8 us
    unnamed x6, local copies, waits for them, and re-layouts  2.91 us

profile of v1, /device:TPU:1, one launch (start us, length us, event | category | flops | bytes accessed | tf_op | source)
XLA Modules:
  0.0 27.6 jit_solution(3785620085845071738)
XLA Ops:
  1.9 0.0 copy-start
  1.9 0.8 %copy-done = bf16[22,1152]{1,0:T(8,128)(2,1)S(1)} copy-done((bf16[22,1152]{1,0:T(8,128)(2,1)S(1)}, bf16[22,1152]{1,0:T(8,128)(2,1)}, u32[]{:S(2)}) %copy-start) | copy-done | bytes 50712
  2.7 0.0 copy-start.1
  2.7 0.8 %copy-done.1 = bf16[22,1152]{1,0:T(8,128)(2,1)S(1)} copy-done((bf16[22,1152]{1,0:T(8,128)(2,1)S(1)}, bf16[22,1152]{1,0:T(8,128)(2,1)}, u32[]{:S(2)}) %copy-start.1) | copy-done | bytes 50712
  3.6 22.8 %shard_map.59 = (f32[22,1152]{1,0:T(8,128)S(1)}, f32[22,1152]{1,0:T(8,128)S(1)}) custom-call(bf16[22,1152]{1,0:T(8,128)(2,1)S(1)} %copy-done, bf16[22,1152]{1,0:T(8,128)(2,1)S(1)} %copy-done.1, f32[1]{0:T(128)} %bitcast.2.scale_ref, f32[1]{0:T(128)} %bitcast.3.bias_ref), custom_call_target="tpu_custom_call" | custom-call | tf_op jit(solution)/shard_map/pallas_call | solution.py:124
  26.3 0.6 %copy.10 = f32[22,1152]{1,0:T(8,128)} copy(f32[22,1152]{1,0:T(8,128)S(1)} %get-tuple-element.4) | data formatting | bytes 202752
  27.0 0.6 %copy.11 = f32[22,1152]{1,0:T(8,128)} copy(f32[22,1152]{1,0:T(8,128)S(1)} %get-tuple-element.5) | data formatting | bytes 202752
Async XLA Ops:
  1.9 0.8 %copy-start = (bf16[22,1152]{1,0:T(8,128)(2,1)S(1)}, bf16[22,1152]{1,0:T(8,128)(2,1)}, u32[]{:S(2)}) copy-start(bf16[22,1152]{1,0:T(8,128)(2,1)} %img_ref.1) | copy-start | bytes 152068
  2.7 0.8 %copy-start.1 = (bf16[22,1152]{1,0:T(8,128)(2,1)S(1)}, bf16[22,1152]{1,0:T(8,128)(2,1)}, u32[]{:S(2)}) copy-start(bf16[22,1152]{1,0:T(8,128)(2,1)} %txt_ref.1) | copy-start | bytes 152068

commit v2 on v1

--- a/solution.py
+++ b/solution.py
@@ -11,8 +11,20 @@
 F32, BF16 = jnp.float32, jnp.bfloat16
 
 
-def unit_rows(x_ref, wide, length_ref, unit_ref):
-    rows = x_ref.shape[0]
+def pack(x):
+    width = x.shape[1]
+    left = -(-width // 256) * 128
+    right = jnp.concatenate([x[16:, left:], jnp.zeros((8, 2 * left - width), x.dtype)], axis=1)
+    return x[:16], jnp.concatenate([x[16:, :left], right], axis=0)
+
+
+def unpack_tail(tail, width):
+    left = tail.shape[1]
+    return jnp.concatenate([tail[:8], tail[8:, :width - left]], axis=1)
+
+
+def unit_rows(x_ref, wide, length_ref, unit_ref, block_ref):
+    rows, width = x_ref.shape
     wide[...] = jnp.zeros_like(wide)
     wide[:rows] = x_ref[...].astype(F32)
     x = wide[...]
@@ -20,7 +32,31 @@
     unit = x / length
     unit_ref[...] = unit
     length_ref[...] = jnp.broadcast_to(length, length_ref.shape)
-    return unit.astype(BF16)
+    head, tail = pack(unit)
+    block_ref[:, :width] = head.astype(BF16)
+    block_ref[:, width:] = tail.astype(BF16)
+
+
+def all_rows(blocks, width):
+    n = blocks.shape[0]
+    heads = blocks[:, :, :width].reshape(n * 16, width)
+    tails = [unpack_tail(blocks[k, :, width:].astype(F32), width) for k in range(n)]
+    return jnp.concatenate([heads, jnp.concatenate(tails, axis=0).astype(BF16)], axis=0)
+
+
+def to_blocks(partial, blocks):
+    n, width = blocks.shape[0], partial.shape[1]
+    for k in range(n):
+        head, tail = pack(jnp.concatenate(
+            [partial[16 * k:16 * k + 16], partial[16 * n + 8 * k:16 * n + 8 * k + 8]], axis=0))
+        blocks[k, :, :width] = head.astype(BF16)
+        blocks[k, :, width:] = tail.astype(BF16)
+
+
+def member_row(index, n):
+    tail = index - 16 * n
+    member = jnp.where(index < 16 * n, index // 16, tail // 8)
+    return member, jnp.where(index < 16 * n, index % 16, 16 + tail % 8)
 
 
 def norm_back(unit, length, upstream):
@@ -29,10 +65,13 @@
 
 
 def kernel(n_row, n_col, cores, img_ref, txt_ref, scale_ref, bias_ref, gimg_ref, gtxt_ref,
-           wide, iu, tu, il, tl, gi, gt, wt, pi, pt, ri, rt,
-           si, ci, st, ct, si2, ci2, st2, ct2):
-    rows = img_ref.shape[0]
-    pad = gi.shape[1]
+           xi, xt, wide, iu, tu, il, tl, gi, gt, wt, pi, pt, ri, rt,
+           in_sem, si, ci, st, ct, si2, ci2, st2, ct2):
+    rows, width = img_ref.shape
+    load_t = pltpu.make_async_copy(txt_ref, xt, in_sem.at[0])
+    load_i = pltpu.make_async_copy(img_ref, xi, in_sem.at[1])
+    load_t.start()
+    load_i.start()
     n_i, n_t = n_row * cores, n_col // cores
     row, col = lax.axis_index("row"), lax.axis_index("col")
     plane, core = col // cores, col % cores
@@ -52,8 +91,10 @@
         pl.semaphore_signal(barrier, inc=1, device_id=at_t(h), device_id_type=MESH)
     for g in to_i:
         pl.semaphore_signal(barrier, inc=1, device_id=at_i(g), device_id_type=MESH)
-    gt[me_t] = unit_rows(txt_ref, wide, tl, tu)
-    gi[me_i] = unit_rows(img_ref, wide, il, iu)
+    load_t.wait()
+    unit_rows(xt, wide, tl, tu, gt.at[me_t])
+    load_i.wait()
+    unit_rows(xi, wide, il, iu, gi.at[me_i])
     pl.semaphore_wait(barrier, n_i + n_t - 2)
 
     def spread(src_of, dst, mine, partners, place, send, recv):
@@ -80,70 +121,80 @@
     for g in to_i:
         arrived(gi, g, ci, si)
 
-    images = gi[...].reshape(n_i * pad, -1)
-    texts = gt[...].reshape(n_t * pad, -1)
+    images = all_rows(gi, width)
+    texts = all_rows(gt, width)
     temperature = jnp.exp(jnp.full((1, 1), scale_ref[0], F32))
     scores = lax.dot_general(images, texts, (((1,), (1,)), ((), ())), preferred_element_type=F32)
     r = lax.broadcasted_iota(jnp.int32, scores.shape, 0)
     c = lax.broadcasted_iota(jnp.int32, scores.shape, 1)
-    g, h = r // pad, c // pad
-    row_ids = ((g // cores) * n_col + plane * cores + g % cores) * rows + r % pad
-    col_ids = ((h * cores + core) * n_row + row) * rows + c % pad
+    g, r = member_row(r, n_i)
+    h, c = member_row(c, n_t)
+    row_ids = ((g // cores) * n_col + plane * cores + g % cores) * rows + r
+    col_ids = ((h * cores + core) * n_row + row) * rows + c
     label = jnp.where(row_ids == col_ids, F32(1.0), F32(-1.0))
     margin = label * (temperature * scores + bias_ref[0])
     weights = -label * jax.nn.sigmoid(-margin)
     wt[...] = weights.T.astype(BF16)
-    pt[...] = jnp.dot(wt[...], images, preferred_element_type=F32).astype(BF16).reshape(pt.shape)
+    to_blocks(jnp.dot(wt[...], images, preferred_element_type=F32), pt)
     sent += spread(lambda h: pt.at[h], rt, me_t, to_t, at_t, st2, ct2)
-    pi[...] = jnp.dot(weights.astype(BF16), texts, preferred_element_type=F32).astype(BF16).reshape(pi.shape)
+    to_blocks(jnp.dot(weights.astype(BF16), texts, preferred_element_type=F32), pi)
     sent += spread(lambda g: pi.at[g], ri, me_i, to_i, at_i, si2, ci2)
+
+    def rows_of(total):
+        return temperature * jnp.concatenate([total[:, :width], unpack_tail(total[:, width:], width)], axis=0)
 
     total = pt[me_t].astype(F32)
     for h in to_t:
         arrived(rt, h, ct2, st2)
         total += rt[h].astype(F32)
-    gtxt_ref[...] = norm_back(tu[...], tl[:, :1], temperature * total)[:rows]
+    gtxt_ref[...] = norm_back(tu[...], tl[:, :1], rows_of(total))[:rows]
     total = pi[me_i].astype(F32)
     for g in to_i:
         arrived(ri, g, ci2, si2)
         total += ri[g].astype(F32)
-    gimg_ref[...] = norm_back(iu[...], il[:, :1], temperature * total)[:rows]
+    gimg_ref[...] = norm_back(iu[...], il[:, :1], rows_of(total))[:rows]
     for copy in sent:
         copy.wait_send()
 
 
 def on_device(n_row, n_col, images, texts, logarithmic_scale, similarity_bias):
     rows, width = images.shape
-    pad = -(-rows // 16) * 16
+    pad = 24
+    packed = width + -(-width // 256) * 128
+    assert 16 < rows <= pad
     cores = 2 if n_col % 2 == 0 else 1
     n_i, n_t = n_row * cores, n_col // cores
     vmem = pl.BlockSpec(memory_space=pltpu.VMEM)
+    hbm = pl.BlockSpec(memory_space=pltpu.HBM)
     smem = pl.BlockSpec(memory_space=pltpu.SMEM)
     out = jax.ShapeDtypeStruct((rows, width), F32)
     dma = pltpu.SemaphoreType.DMA
     return pl.pallas_call(
         functools.partial(kernel, n_row, n_col, cores),
         out_shape=(out, out),
-        in_specs=[vmem, vmem, smem, smem],
+        in_specs=[hbm, hbm, smem, smem],
         out_specs=(vmem, vmem),
         scratch_shapes=[
+            pltpu.VMEM((rows, width), BF16),
+            pltpu.VMEM((rows, width), BF16),
             pltpu.VMEM((pad, width), F32),
             pltpu.VMEM((pad, width), F32),
             pltpu.VMEM((pad, width), F32),
             pltpu.VMEM((pad, 128), F32),
             pltpu.VMEM((pad, 128), F32),
-            pltpu.VMEM((n_i, pad, width), BF16),
-            pltpu.VMEM((n_t, pad, width), BF16),
+            pltpu.VMEM((n_i, 16, packed), BF16),
+            pltpu.VMEM((n_t, 16, packed), BF16),
             pltpu.VMEM((n_t * pad, n_i * pad), BF16),
-            pltpu.VMEM((n_i, pad, width), BF16),
-            pltpu.VMEM((n_t, pad, width), BF16),
-            pltpu.VMEM((n_i, pad, width), BF16),
-            pltpu.VMEM((n_t, pad, width), BF16),
+            pltpu.VMEM((n_i, 16, packed), BF16),
+            pltpu.VMEM((n_t, 16, packed), BF16),
+            pltpu.VMEM((n_i, 16, packed), BF16),
+            pltpu.VMEM((n_t, 16, packed), BF16),
+            dma((2,)),
             dma((n_i,)), dma((n_i,)), dma((n_t,)), dma((n_t,)),
             dma((n_i,)), dma((n_i,)), dma((n_t,)), dma((n_t,)),
         ],
         compiler_params=pltpu.CompilerParams(
-            collective_id=0, has_side_effects=True, vmem_limit_bytes=48 * 2**20),
+            collective_id=0, has_side_effects=True),
     )(images, texts, logarithmic_scale.reshape(1), similarity_bias.reshape(1))
 
 

time: 27.9 us -> 25 us (0.90)
  Pallas kernels: 22.8 us -> 20.6 us
  local copies, waits for them, and re-layouts: 2.91 us -> 2.23 us
    pallas_call x1, Pallas kernels: 22.8 us -> 20.6 us  [on_device(): pl.pallas_call(functools.partial(kernel, n_row, n_col, cores), out_shape=...]
    unnamed x6 -> x4, local copies, waits for them, and re-layouts: 2.91 us -> 2.23 us
where the time goes in v2:
time: 25 us; the launch traced here: 24.8 us
  Pallas kernels  20.6 us (82%)
  local copies, waits for them, and re-layouts  2.23 us (9%)
  between operations  1.94 us (8%)
    pallas_call x1, Pallas kernels, on_device(): pl.pallas_call(functools.partial(kernel, n_row, n_col, cores), out_shape=...  20.6 us
    unnamed x4, local copies, waits for them, and re-layouts  2.23 us

profile of v2, /device:TPU:1, one launch (start us, length us, event | category | flops | bytes accessed | tf_op | source)
XLA Modules:
  0.0 24.8 jit_solution(10243615797001902234)
XLA Ops:
  1.9 20.6 %shard_map.59 = (f32[22,1152]{1,0:T(8,128)}, f32[22,1152]{1,0:T(8,128)}) custom-call(bf16[22,1152]{1,0:T(8,128)(2,1)} %img_ref.1, bf16[22,1152]{1,0:T(8,128)(2,1)} %txt_ref.1, f32[1]{0:T(128)} %bitcast.2.scale_ref, f32[1]{0:T(128)} %bitcast.3.bias_ref), custom_call_target="tpu_custom_call" | custom-call | tf_op jit(solution)/shard_map/pallas_call | solution.py:172
  22.5 0.0 copy-start
  22.5 1.6 %copy.10 = f32[22,1152]{1,0:T(8,128)} copy(f32[22,1152]{1,0:T(8,128)} %get-tuple-element.4) | data formatting | bytes 202752
  24.1 0.0 copy-done
  24.1 0.6 %copy.11 = f32[22,1152]{1,0:T(8,128)} copy(f32[22,1152]{1,0:T(8,128)S(1)} %copy-done) | data formatting | bytes 202752
Async XLA Ops:
  22.5 1.6 %copy-start = (f32[22,1152]{1,0:T(8,128)S(1)}, f32[22,1152]{1,0:T(8,128)}, u32[]{:S(2)}) copy-start(f32[22,1152]{1,0:T(8,128)} %get-tuple-element.5) | copy-start | bytes 304132

commit v3 on v2

v3 whole, which is shorter than its diff:
```python
import functools

import jax
import jax.numpy as jnp
from jax import lax
from jax.experimental import pallas as pl
from jax.experimental.pallas import tpu as pltpu
from jax.sharding import PartitionSpec as P

MESH = pl.DeviceIdType.MESH
F32, BF16 = jnp.float32, jnp.bfloat16


def pack(x):
    width = x.shape[1]
    left = -(-width // 256) * 128
    right = jnp.concatenate([x[16:, left:], jnp.zeros((8, 2 * left - width), x.dtype)], axis=1)
    return x[:16], jnp.concatenate([x[16:, :left], right], axis=0)


def unpack_tail(tail, width):
    left = tail.shape[1]
    return jnp.concatenate([tail[:8], tail[8:, :width - left]], axis=1)


def unit_rows(x_ref, wide, length_ref, unit_ref, block_ref):
    rows, width = x_ref.shape
    wide[...] = jnp.zeros_like(wide)
    wide[:rows] = x_ref[...].astype(F32)
    x = wide[...]
    length = jnp.sqrt(jnp.sum(x * x, axis=1, keepdims=True) + 1e-06)
    unit = x / length
    unit_ref[...] = unit
    length_ref[...] = jnp.broadcast_to(length, length_ref.shape)
    head, tail = pack(unit)
    block_ref[:, :width] = head.astype(BF16)
    block_ref[:, width:] = tail.astype(BF16)


def all_rows(blocks, width):
    n = blocks.shape[0]
    heads = blocks[:, :, :width].reshape(n * 16, width)
    tails = [unpack_tail(blocks[k, :, width:].astype(F32), width) for k in range(n)]
    return jnp.concatenate([heads, jnp.concatenate(tails, axis=0).astype(BF16)], axis=0)


def to_blocks(partial, blocks):
    n, width = blocks.shape[0], partial.shape[1]
    for k in range(n):
        head, tail = pack(jnp.concatenate(
            [partial[16 * k:16 * k + 16], partial[16 * n + 8 * k:16 * n + 8 * k + 8]], axis=0))
        blocks[k, :, :width] = head.astype(blocks.dtype)
        blocks[k, :, width:] = tail.astype(blocks.dtype)


def member_row(index, n):
    tail = index - 16 * n
    member = jnp.where(index < 16 * n, index // 16, tail // 8)
    return member, jnp.where(index < 16 * n, index % 16, 16 + tail % 8)


def norm_back(unit, length, upstream):
    along = jnp.sum(unit * upstream, axis=1, keepdims=True)
    return (upstream - unit * along) / length


def kernel(n_row, n_t, img_ref, txt_ref, scale_ref, bias_ref, gimg_ref, gtxt_ref,
           xi, xt, wide, iu, tu, il, tl, gi, gt, wt, wh, wl, pt, ps, po, pi, acc, rt, rl, rs, ri,
           in_sem, send_sem, ci, ct, ct2, ci2, pair_sem):
    rows, width = img_ref.shape
    load_t = pltpu.make_async_copy(txt_ref, xt, in_sem.at[0])
    load_i = pltpu.make_async_copy(img_ref, xi, in_sem.at[1])
    load_t.start()
    load_i.start()
    n_i = 2 * n_row
    row, col = lax.axis_index("row"), lax.axis_index("col")
    plane, core = col // 2, col % 2
    other_core = 1 - core
    me_i = core * n_row + row
    line = n_t == 4
    first_end, last_end = plane == 0, plane == n_t - 1
    relay = jnp.logical_or(plane == 1, plane == 2)
    far_end = jnp.where(plane == 1, 3, 0)
    near_end = jnp.where(plane == 1, 0, 3)

    def at_row(r):
        return (r, col)

    def at_plane(h):
        return (row, 2 * h + core)

    sibling = (row, 2 * plane + other_core)
    other_rows = [lax.rem(row + k, n_row) for k in range(1, n_row)]
    planes = {k: lax.rem(plane + k, n_t) for k in range(1, n_t)}
    order = [2, 3, 1] if line else list(planes)

    barrier = pltpu.get_barrier_semaphore()
    for place in [at_plane(planes[k]) for k in order] + [at_row(r) for r in other_rows] + [sibling]:
        pl.semaphore_signal(barrier, inc=1, device_id=place, device_id_type=MESH)
    load_t.wait()
    unit_rows(xt, wide, tl, tu, gt.at[plane])
    load_i.wait()
    unit_rows(xi, wide, il, iu, gi.at[me_i])
    pl.semaphore_wait(barrier, n_row + n_t - 1)

    sent = []

    def when(condition):
        return pl.when(condition) if condition is not None else lambda f: f()

    def push(src, dst, recv, place, condition=None):
        slot = send_sem.at[len(sent)]

        def copy():
            return pltpu.make_async_remote_copy(
                src_ref=src, dst_ref=dst, send_sem=slot, recv_sem=recv,
                device_id=place, device_id_type=MESH)

        when(condition)(lambda: copy().start())
        sent.append((copy, condition))

    def arrived(dst, recv, condition=None):
        when(condition)(lambda: pltpu.make_async_remote_copy(
            src_ref=dst, dst_ref=dst, send_sem=send_sem.at[0], recv_sem=recv,
            device_id=sibling, device_id_type=MESH).wait_recv())

    def direct(k):
        if not line or k == 2:
            return None
        return jnp.logical_not(last_end if k == 1 else first_end)

    for k in order:
        push(gt.at[plane], gt.at[plane], ct.at[plane], at_plane(planes[k]), direct(k))
    for r in other_rows:
        push(gi.at[me_i], gi.at[me_i], ci.at[me_i], at_row(r))
    push(gi.at[me_i], gi.at[me_i], ci.at[me_i], sibling)
    for k, r in enumerate(other_rows):
        g = core * n_row + r
        arrived(gi.at[g], ci.at[g])
        push(gi.at[g], gi.at[g], ci.at[g], sibling)
        if line and k == 0:
            h = planes[2]
            arrived(gt.at[h], ct.at[h])
            push(gt.at[far_end], gt.at[far_end], ct.at[far_end], at_plane(near_end), relay)
    for k in order:
        if not (line and k == 2):
            arrived(gt.at[planes[k]], ct.at[planes[k]])
    for r in [row] + other_rows:
        g = other_core * n_row + r
        arrived(gi.at[g], ci.at[g])

    images = all_rows(gi, width)
    texts = all_rows(gt, width)
    temperature = jnp.exp(jnp.full((1, 1), scale_ref[0], F32))
    scores = lax.dot_general(images, texts, (((1,), (1,)), ((), ())), preferred_element_type=F32)
    r = lax.broadcasted_iota(jnp.int32, scores.shape, 0)
    c = lax.broadcasted_iota(jnp.int32, scores.shape, 1)
    g, r = member_row(r, n_i)
    h, c = member_row(c, n_t)
    row_ids = ((g % n_row) * (2 * n_t) + plane * 2 + g // n_row) * rows + r
    col_ids = ((h * 2 + core) * n_row + row) * rows + c
    label = jnp.where(row_ids == col_ids, F32(1.0), F32(-1.0))
    margin = label * (temperature * scores + bias_ref[0])
    weights = -label * jax.nn.sigmoid(-margin)
    wt[...] = weights.T.astype(BF16)
    wh[...] = weights[:16 * n_i].astype(BF16)
    wl[...] = weights[16 * n_i:].astype(BF16)

    to_blocks(jnp.dot(wt[...], images, preferred_element_type=F32), pt)
    if line:
        end = jnp.logical_or(first_end, last_end)
        opposite = jnp.where(first_end, 3, 0)
        push(pt.at[opposite], rl, pair_sem.at[1], at_plane(jnp.where(first_end, 1, 2)), end)
        through = jnp.logical_not(relay)
    for k in order:
        push(pt.at[planes[k]], rt.at[plane], ct2.at[plane], at_plane(planes[k]),
             through if line and k == 2 else direct(k))

    def half(c):
        head = wh[pl.ds(pl.multiple_of(c * (16 * n_row), 16), 16 * n_row)]
        tail = wl[pl.ds(pl.multiple_of(c * (8 * n_row), 16), 8 * n_row)]
        return jnp.dot(jnp.concatenate([head, tail], axis=0), texts, preferred_element_type=F32)

    to_blocks(half(other_core), ps)
    push(ps, rs, pair_sem.at[0], sibling)
    to_blocks(half(core), po)
    arrived(rs, pair_sem.at[0])
    for r in other_rows:
        pi[r] = (po[r] + rs[r].astype(F32)).astype(BF16)
        push(pi.at[r], ri.at[row], ci2.at[row], at_row(r))
    if line:
        @pl.when(relay)
        def _():
            arrived(rl, pair_sem.at[1])
            pt[far_end] = (pt[far_end].astype(F32) + rl[...].astype(F32)).astype(BF16)
        push(pt.at[far_end], rt.at[plane], ct2.at[plane], at_plane(far_end), relay)

    def rows_of(total):
        return temperature * jnp.concatenate([total[:, :width], unpack_tail(total[:, width:], width)], axis=0)

    acc[...] = po[row] + rs[row].astype(F32)
    for r in other_rows:
        arrived(ri.at[r], ci2.at[r])
        acc[...] += ri[r].astype(F32)
    gimg_ref[...] = norm_back(iu[...], il[:, :1], rows_of(acc[...]))[:rows]
    acc[...] = pt[plane].astype(F32)
    for k in order[1:] + order[:1]:
        h = planes[k]

        def add(h=h):
            arrived(rt.at[h], ct2.at[h])
            acc[...] += rt[h].astype(F32)

        when(direct(k))(add)
    gtxt_ref[...] = norm_back(tu[...], tl[:, :1], rows_of(acc[...]))[:rows]
    for copy, condition in sent:
        when(condition)(lambda copy=copy: copy().wait_send())


def on_device(n_row, n_col, images, texts, logarithmic_scale, similarity_bias):
    rows, width = images.shape
    pad = 24
    packed = width + -(-width // 256) * 128
    assert 16 < rows <= pad and n_col % 2 == 0 and n_row % 2 == 0
    n_i, n_t = 2 * n_row, n_col // 2
    vmem = pl.BlockSpec(memory_space=pltpu.VMEM)
    hbm = pl.BlockSpec(memory_space=pltpu.HBM)
    smem = pl.BlockSpec(memory_space=pltpu.SMEM)
    out = jax.ShapeDtypeStruct((rows, width), F32)
    dma = pltpu.SemaphoreType.DMA

    def blocks(n, kind=BF16):
        return pltpu.VMEM((n, 16, packed), kind)

    return pl.pallas_call(
        functools.partial(kernel, n_row, n_t),
        out_shape=(out, out),
        in_specs=[hbm, hbm, smem, smem],
        out_specs=(vmem, vmem),
        scratch_shapes=[
            pltpu.VMEM((rows, width), BF16),
            pltpu.VMEM((rows, width), BF16),
            pltpu.VMEM((pad, width), F32),
            pltpu.VMEM((pad, width), F32),
            pltpu.VMEM((pad, width), F32),
            pltpu.VMEM((pad, 128), F32),
            pltpu.VMEM((pad, 128), F32),
            blocks(n_i),
            blocks(n_t),
            pltpu.VMEM((n_t * pad, n_i * pad), BF16),
            pltpu.VMEM((n_i * 16, n_t * pad), BF16),
            pltpu.VMEM((n_i * 8, n_t * pad), BF16),
            blocks(n_t),
            blocks(n_row),
            blocks(n_row, F32),
            blocks(n_row),
            pltpu.VMEM((16, packed), F32),
            blocks(n_t),
            pltpu.VMEM((16, packed), BF16),
            blocks(n_row),
            blocks(n_row),
            dma((2,)), dma((3 * n_row + 2 * n_t + 2,)),
            dma((n_i,)), dma((n_t,)), dma((n_t,)), dma((n_row,)), dma((2,)),
        ],
        compiler_params=pltpu.CompilerParams(
            collective_id=0, has_side_effects=True),
    )(images, texts, logarithmic_scale.reshape(1), similarity_bias.reshape(1))


def solution(mesh):
    return jax.shard_map(
        functools.partial(on_device, mesh.shape["row"], mesh.shape["col"]),
        mesh=mesh,
        in_specs=(P(("row", "col"), None), P(("col", "row"), None), P(), P()),
        out_specs=(P(("row", "col"), None), P(("col", "row"), None)),
        check_vma=False,
    )
```

time: 25 us -> 25.2 us (level)
  the two profiles are of different devices: /device:TPU:1 before, /device:TPU:0 now
where the time goes in v3:
time: 25.2 us; the launch traced here: 25 us
  Pallas kernels  20.8 us (83%)
  local copies, waits for them, and re-layouts  2.23 us (9%)
  between operations  1.94 us (8%)
    pallas_call x1, Pallas kernels, on_device(): pl.pallas_call(functools.partial(kernel, n_row, n_t), out_shape=(out, out...  20.8 us
    unnamed x4, local copies, waits for them, and re-layouts  2.23 us

profile of v3, /device:TPU:0, one launch (start us, length us, event | category | flops | bytes accessed | tf_op | source)
XLA Modules:
  0.0 25.0 jit_solution(2662103943443949204)
XLA Ops:
  1.9 20.8 %shard_map.59 = (f32[22,1152]{1,0:T(8,128)}, f32[22,1152]{1,0:T(8,128)}) custom-call(bf16[22,1152]{1,0:T(8,128)(2,1)} %img_ref.1, bf16[22,1152]{1,0:T(8,128)(2,1)} %txt_ref.1, f32[1]{0:T(128)} %bitcast.2.scale_ref, f32[1]{0:T(128)} %bitcast.3.bias_ref), custom_call_target="tpu_custom_call" | custom-call | tf_op jit(solution)/shard_map/pallas_call | solution.py:235
  22.7 0.0 copy-start
  22.7 1.6 %copy.10 = f32[22,1152]{1,0:T(8,128)} copy(f32[22,1152]{1,0:T(8,128)} %get-tuple-element.4) | data formatting | bytes 202752
  24.3 0.0 copy-done
  24.3 0.6 %copy.11 = f32[22,1152]{1,0:T(8,128)} copy(f32[22,1152]{1,0:T(8,128)S(1)} %copy-done) | data formatting | bytes 202752
Async XLA Ops:
  22.7 1.6 %copy-start = (f32[22,1152]{1,0:T(8,128)S(1)}, f32[22,1152]{1,0:T(8,128)}, u32[]{:S(2)}) copy-start(f32[22,1152]{1,0:T(8,128)} %get-tuple-element.5) | copy-start | bytes 304132

commit v4 on v3

v4 whole, which is shorter than its diff:
```python
import functools

import jax
import jax.numpy as jnp
from jax import lax
from jax.experimental import pallas as pl
from jax.experimental.pallas import tpu as pltpu
from jax.sharding import PartitionSpec as P

MESH = pl.DeviceIdType.MESH
F32, BF16 = jnp.float32, jnp.bfloat16


def pack(x):
    width = x.shape[1]
    left = -(-width // 256) * 128
    right = jnp.concatenate([x[16:, left:], jnp.zeros((8, 2 * left - width), x.dtype)], axis=1)
    return x[:16], jnp.concatenate([x[16:, :left], right], axis=0)


def unpack_tail(tail, width):
    left = tail.shape[1]
    return jnp.concatenate([tail[:8], tail[8:, :width - left]], axis=1)


def unit_rows(x):
    length = jnp.sqrt(jnp.sum(x * x, axis=1, keepdims=True) + 1e-06)
    return x * (1.0 / length), length


def to_blocks(partial, blocks):
    width = partial.shape[1]
    for k in range(blocks.shape[0]):
        head, tail = pack(partial[24 * k:24 * k + 24])
        blocks[k, :, :width] = head.astype(blocks.dtype)
        blocks[k, :, width:] = tail.astype(blocks.dtype)


def member_row(index):
    member = lax.shift_right_logical(index * 43691, jnp.full_like(index, 20))
    return member, index - 24 * member


def norm_back(unit, length, upstream):
    along = jnp.sum(unit * upstream, axis=1, keepdims=True)
    return (upstream - unit * along) / length


def kernel(n_row, n_t, img_ref, txt_ref, scale_ref, bias_ref, gimg_ref, gtxt_ref,
           oi, ot, iu, tu, il, tl, gi, gt, wt, w, pt, ps, po, pi, acc, rt, rl, rs, ri,
           in_sem, out_sem, send_sem, ci, ct, ct2, ci2, pair_sem):
    rows, width = img_ref.shape
    n_i = 2 * n_row
    row, col = lax.axis_index("row"), lax.axis_index("col")
    plane, core = col // 2, col % 2
    other_core = 1 - core
    me_i = core * n_row + row
    line = n_t == 4
    first_end, last_end = plane == 0, plane == n_t - 1
    relay = jnp.logical_or(plane == 1, plane == 2)
    far_end = jnp.where(plane == 1, 3, 0)
    near_end = jnp.where(plane == 1, 0, 3)

    def at_row(r):
        return (r, col)

    def at_plane(h):
        return (row, 2 * h + core)

    sibling = (row, 2 * plane + other_core)
    other_rows = [lax.rem(row + k, n_row) for k in range(1, n_row)]
    planes = {k: lax.rem(plane + k, n_t) for k in range(1, n_t)}
    order = [2, 3, 1] if line else list(planes)

    barrier = pltpu.get_barrier_semaphore()
    for place in [at_plane(planes[k]) for k in order] + [at_row(r) for r in other_rows] + [sibling]:
        pl.semaphore_signal(barrier, inc=1, device_id=place, device_id_type=MESH)
    load_t = pltpu.make_async_copy(txt_ref, gt.at[plane], in_sem.at[0])
    load_i = pltpu.make_async_copy(img_ref, gi.at[me_i], in_sem.at[1])
    load_t.start()
    load_i.start()
    iu[...] = jnp.zeros_like(iu)
    tu[...] = jnp.zeros_like(tu)
    pl.semaphore_wait(barrier, n_row + n_t - 1)

    sent = []

    def when(condition):
        return pl.when(condition) if condition is not None else lambda f: f()

    def push(src, dst, recv, place, condition=None):
        slot = send_sem.at[len(sent)]

        def copy():
            return pltpu.make_async_remote_copy(
                src_ref=src, dst_ref=dst, send_sem=slot, recv_sem=recv,
                device_id=place, device_id_type=MESH)

        when(condition)(lambda: copy().start())
        sent.append((copy, condition))

    def arrived(dst, recv, condition=None):
        when(condition)(lambda: pltpu.make_async_remote_copy(
            src_ref=dst, dst_ref=dst, send_sem=send_sem.at[0], recv_sem=recv,
            device_id=sibling, device_id_type=MESH).wait_recv())

    def direct(k):
        if not line or k == 2:
            return None
        return jnp.logical_not(last_end if k == 1 else first_end)

    for k in order:
        push(txt_ref, gt.at[plane], ct.at[plane], at_plane(planes[k]), direct(k))
    for r in other_rows:
        push(img_ref, gi.at[me_i], ci.at[me_i], at_row(r))
    push(img_ref, gi.at[me_i], ci.at[me_i], sibling)

    def normalise(blocks, g, units, length_ref=None):
        at = pl.multiple_of(g * 24, 8)
        units[pl.ds(at, rows)] = blocks[g].astype(F32)
        unit, length = unit_rows(units[pl.ds(at, 24)])
        units[pl.ds(at, 24)] = unit
        if length_ref is not None:
            length_ref[...] = jnp.broadcast_to(length, length_ref.shape)

    load_t.wait()
    normalise(gt, plane, tu, tl)
    load_i.wait()
    normalise(gi, me_i, iu, il)
    for k, r in enumerate(other_rows):
        g = core * n_row + r
        arrived(gi.at[g], ci.at[g])
        push(gi.at[g], gi.at[g], ci.at[g], sibling)
        if line and k == 0:
            h = planes[2]
            arrived(gt.at[h], ct.at[h])
            push(gt.at[far_end], gt.at[far_end], ct.at[far_end], at_plane(near_end), relay)
    for r in other_rows:
        normalise(gi, core * n_row + r, iu)
    for r in [row] + other_rows:
        g = other_core * n_row + r
        arrived(gi.at[g], ci.at[g])
        normalise(gi, g, iu)
    images = iu[...].astype(BF16)
    for k in order:
        if not (line and k == 2):
            arrived(gt.at[planes[k]], ct.at[planes[k]])
        normalise(gt, planes[k], tu)
    texts = tu[...].astype(BF16)
    temperature = jnp.exp(jnp.full((1, 1), scale_ref[...], F32))
    scores = lax.dot_general(images, texts, (((1,), (1,)), ((), ())), preferred_element_type=F32)
    r = lax.broadcasted_iota(jnp.int32, (scores.shape[0], 1), 0)
    c = lax.broadcasted_iota(jnp.int32, (1, scores.shape[1]), 1)
    g, r = member_row(r)
    h, c = member_row(c)
    pair = jnp.where(g < n_row, 0, 1)
    row_ids = ((g - pair * n_row) * (2 * n_t) + plane * 2 + pair) * rows + r
    col_ids = ((h * 2 + core) * n_row + row) * rows + c
    label = jnp.where(row_ids == col_ids, F32(1.0), F32(-1.0))
    margin = label * (temperature * scores + bias_ref[...])
    weights = -label * jax.nn.sigmoid(-margin)
    wt[...] = weights.T.astype(BF16)
    w[...] = weights.astype(BF16)

    to_blocks(jnp.dot(wt[...], images, preferred_element_type=F32), pt)
    if line:
        end = jnp.logical_or(first_end, last_end)
        opposite = jnp.where(first_end, 3, 0)
        push(pt.at[opposite], rl, pair_sem.at[1], at_plane(jnp.where(first_end, 1, 2)), end)
        through = jnp.logical_not(relay)
    for k in order:
        push(pt.at[planes[k]], rt.at[plane], ct2.at[plane], at_plane(planes[k]),
             through if line and k == 2 else direct(k))

    def half(c):
        some = w[pl.ds(pl.multiple_of(c * (24 * n_row), 16), 24 * n_row)]
        return jnp.dot(some, texts, preferred_element_type=F32)

    to_blocks(half(other_core), ps)
    push(ps, rs, pair_sem.at[0], sibling)
    to_blocks(half(core), po)
    arrived(rs, pair_sem.at[0])
    for r in other_rows:
        pi[r] = (po[r] + rs[r].astype(F32)).astype(BF16)
        push(pi.at[r], ri.at[row], ci2.at[row], at_row(r))
    if line:
        @pl.when(relay)
        def _():
            arrived(rl, pair_sem.at[1])
            pt[far_end] = (pt[far_end].astype(F32) + rl[...].astype(F32)).astype(BF16)
        push(pt.at[far_end], rt.at[plane], ct2.at[plane], at_plane(far_end), relay)

    def rows_of(total):
        return temperature * jnp.concatenate([total[:, :width], unpack_tail(total[:, width:], width)], axis=0)

    acc[...] = po[row] + rs[row].astype(F32)
    for r in other_rows:
        arrived(ri.at[r], ci2.at[r])
        acc[...] += ri[r].astype(F32)
    oi[...] = norm_back(iu[pl.ds(pl.multiple_of(me_i * 24, 8), 24)], il[:, :1], rows_of(acc[...]))[:rows]
    out_i = pltpu.make_async_copy(oi, gimg_ref, out_sem.at[0])
    out_i.start()
    acc[...] = pt[plane].astype(F32)
    for k in order[1:] + order[:1]:
        h = planes[k]

        def add(h=h):
            arrived(rt.at[h], ct2.at[h])
            acc[...] += rt[h].astype(F32)

        when(direct(k))(add)
    ot[...] = norm_back(tu[pl.ds(pl.multiple_of(plane * 24, 8), 24)], tl[:, :1], rows_of(acc[...]))[:rows]
    out_t = pltpu.make_async_copy(ot, gtxt_ref, out_sem.at[1])
    out_t.start()
    for copy, condition in sent:
        when(condition)(lambda copy=copy: copy().wait_send())
    out_i.wait()
    out_t.wait()


def hand_over(gimg_ref, gtxt_ref, images_ref, texts_ref, sem):
    copies = [pltpu.make_async_copy(gimg_ref, images_ref, sem.at[0]),
              pltpu.make_async_copy(gtxt_ref, texts_ref, sem.at[1])]
    for copy in copies:
        copy.start()
    for copy in copies:
        copy.wait()


def on_device(n_row, n_col, images, texts, logarithmic_scale, similarity_bias):
    rows, width = images.shape
    pad = 24
    packed = width + -(-width // 256) * 128
    assert 16 < rows <= pad and n_col % 2 == 0 and n_row % 2 == 0
    n_i, n_t = 2 * n_row, n_col // 2
    hbm = pl.BlockSpec(memory_space=pl.ANY)
    smem = pl.BlockSpec(memory_space=pltpu.SMEM)
    out = jax.ShapeDtypeStruct((rows, width), F32)
    dma = pltpu.SemaphoreType.DMA

    def blocks(n, kind=BF16):
        return pltpu.VMEM((n, 16, packed), kind)

    grads = pl.pallas_call(
        functools.partial(kernel, n_row, n_t),
        out_shape=(out, out),
        in_specs=[hbm, hbm, smem, smem],
        out_specs=(hbm, hbm),
        scratch_shapes=[
            pltpu.VMEM((rows, width), F32),
            pltpu.VMEM((rows, width), F32),
            pltpu.VMEM((n_i * pad, width), F32),
            pltpu.VMEM((n_t * pad, width), F32),
            pltpu.VMEM((pad, 128), F32),
            pltpu.VMEM((pad, 128), F32),
            pltpu.VMEM((n_i, rows, width), BF16),
            pltpu.VMEM((n_t, rows, width), BF16),
            pltpu.VMEM((n_t * pad, n_i * pad), BF16),
            pltpu.VMEM((n_i * pad, n_t * pad), BF16),
            blocks(n_t),
            blocks(n_row),
            blocks(n_row, F32),
            blocks(n_row),
            pltpu.VMEM((16, packed), F32),
            blocks(n_t),
            pltpu.VMEM((16, packed), BF16),
            blocks(n_row),
            blocks(n_row),
            dma((2,)), dma((2,)), dma((3 * n_row + 2 * n_t + 2,)),
            dma((n_i,)), dma((n_t,)), dma((n_t,)), dma((n_row,)), dma((2,)),
        ],
        compiler_params=pltpu.CompilerParams(
            collective_id=0, has_side_effects=True),
    )(images, texts, logarithmic_scale, similarity_bias)
    return pl.pallas_call(
        hand_over,
        out_shape=(out, out),
        in_specs=[hbm, hbm],
        out_specs=(hbm, hbm),
        scratch_shapes=[dma((2,))],
    )(*grads)


def solution(mesh):
    return jax.shard_map(
        functools.partial(on_device, mesh.shape["row"], mesh.shape["col"]),
        mesh=mesh,
        in_specs=(P(("row", "col"), None), P(("col", "row"), None), P(), P()),
        out_specs=(P(("row", "col"), None), P(("col", "row"), None)),
        check_vma=False,
    )
```

time: 25.2 us -> 31.2 us (1.24)
  Pallas kernels: 20.8 us -> 29.1 us
  local copies, waits for them, and re-layouts: 2.23 us -> 0 us
    pallas_call x0 -> x1, Pallas kernels: none -> 7.82 us  [on_device(): pl.pallas_call(hand_over, out_shape=(out, out), in_specs=[hbm, hbm], out_...]
    unnamed x4 -> x0, local copies, waits for them, and re-layouts: 2.23 us -> none
    pallas_call x1, Pallas kernels: 20.8 us -> 21.3 us  [on_device(): pl.pallas_call(functools.partial(kernel, n_row, n_t), out_shape=(out, out...]
where the time goes in v4:
time: 31.2 us; the launch traced here: 31 us
  Pallas kernels  29.1 us (93%)
  between operations  1.93 us (6%)
    pallas_call x1, Pallas kernels, on_device(): pl.pallas_call(functools.partial(kernel, n_row, n_t), out_shape=(out, out...  21.3 us
    pallas_call x1, Pallas kernels, on_device(): pl.pallas_call(hand_over, out_shape=(out, out), in_specs=[hbm, hbm], out_...  7.82 us

profile of v4, /device:TPU:0, one launch (start us, length us, event | category | flops | bytes accessed | tf_op | source)
XLA Modules:
  0.0 31.0 jit_solution(3380373738528997510)
XLA Ops:
  1.9 21.3 %shard_map.59 = (f32[22,1152]{1,0:T(8,128)}, f32[22,1152]{1,0:T(8,128)}) custom-call(bf16[22,1152]{1,0:T(8,128)(2,1)} %img_ref.1, bf16[22,1152]{1,0:T(8,128)(2,1)} %txt_ref.1, f32[]{:T(128)S(6)} %copy.6.scale_ref, f32[]{:T(128)S(6)} %copy.7.bias_ref), custom_call_target="tpu_custom_call" | custom-call | tf_op jit(solution)/shard_map/pallas_call | solution.py:244
  23.2 7.8 %shard_map.60 = (f32[22,1152]{1,0:T(8,128)}, f32[22,1152]{1,0:T(8,128)}) custom-call(f32[22,1152]{1,0:T(8,128)} %get-tuple-element.4.gimg_ref, f32[22,1152]{1,0:T(8,128)} %get-tuple-element.5.gtxt_ref), custom_call_target="tpu_custom_call" | custom-call | tf_op jit(solution)/shard_map/pallas_call | solution.py:275

commit v5 on v3

v5 whole, which is shorter than its diff:
```python
import functools

import jax
import jax.numpy as jnp
from jax import lax
from jax.experimental import pallas as pl
from jax.experimental.pallas import tpu as pltpu
from jax.sharding import PartitionSpec as P

MESH = pl.DeviceIdType.MESH
F32, BF16 = jnp.float32, jnp.bfloat16


def pack(x):
    width = x.shape[1]
    left = -(-width // 256) * 128
    right = jnp.concatenate([x[16:, left:], jnp.zeros((8, 2 * left - width), x.dtype)], axis=1)
    return x[:16], jnp.concatenate([x[16:, :left], right], axis=0)


def unpack_tail(tail, width):
    left = tail.shape[1]
    return jnp.concatenate([tail[:8], tail[8:, :width - left]], axis=1)


def unit_rows(x_ref, wide, length_ref, unit_ref, block_ref):
    rows, width = x_ref.shape
    wide[...] = jnp.zeros_like(wide)
    wide[:rows] = x_ref[...].astype(F32)
    x = wide[...]
    length = jnp.sqrt(jnp.sum(x * x, axis=1, keepdims=True) + 1e-06)
    unit = x / length
    unit_ref[...] = unit
    length_ref[...] = jnp.broadcast_to(length, length_ref.shape)
    head, tail = pack(unit)
    block_ref[:, :width] = head.astype(BF16)
    block_ref[:, width:] = tail.astype(BF16)


def all_rows(blocks, width):
    n = blocks.shape[0]
    heads = blocks[:, :, :width].reshape(n * 16, width)
    tails = [unpack_tail(blocks[k, :, width:].astype(F32), width) for k in range(n)]
    return jnp.concatenate([heads, jnp.concatenate(tails, axis=0).astype(BF16)], axis=0)


def to_blocks(partial, blocks):
    n, width = blocks.shape[0], partial.shape[1]
    for k in range(n):
        head, tail = pack(jnp.concatenate(
            [partial[16 * k:16 * k + 16], partial[16 * n + 8 * k:16 * n + 8 * k + 8]], axis=0))
        blocks[k, :, :width] = head.astype(blocks.dtype)
        blocks[k, :, width:] = tail.astype(blocks.dtype)


def member_row(index, n):
    tail = index - 16 * n
    member = jnp.where(index < 16 * n, index // 16, tail // 8)
    return member, jnp.where(index < 16 * n, index % 16, 16 + tail % 8)


def norm_back(unit, length, upstream):
    along = jnp.sum(unit * upstream, axis=1, keepdims=True)
    return (upstream - unit * along) / length


def kernel(n_row, n_t, img_ref, txt_ref, scale_ref, bias_ref, gimg_ref, gtxt_ref,
           xi, xt, wide, iu, tu, il, tl, gi, gt, label_ref, wt, wh, wl, pt, ps, po, pi, acc, rt, rs, ri,
           in_sem, send_sem, ci, ct, ct2, ci2, pair_sem):
    rows, width = img_ref.shape
    load_t = pltpu.make_async_copy(txt_ref, xt, in_sem.at[0])
    load_i = pltpu.make_async_copy(img_ref, xi, in_sem.at[1])
    load_t.start()
    load_i.start()
    n_i = 2 * n_row
    row, col = lax.axis_index("row"), lax.axis_index("col")
    plane, core = col // 2, col % 2
    other_core = 1 - core
    me_i = core * n_row + row
    low = plane < n_t // 2
    from_end = jnp.where(low, plane, n_t - 1 - plane)
    planes = []
    for t in range(n_t - 1, 0, -1):
        t = jnp.where(t > from_end, t, t - 1)
        planes.append(jnp.where(low, t, n_t - 1 - t))

    def at_row(r):
        return (r, col)

    def at_plane(h):
        return (row, 2 * h + core)

    sibling = (row, 2 * plane + other_core)
    other_rows = [lax.rem(row + k, n_row) for k in range(1, n_row)]

    barrier = pltpu.get_barrier_semaphore()
    for place in [at_plane(h) for h in planes] + [at_row(r) for r in other_rows] + [sibling]:
        pl.semaphore_signal(barrier, inc=1, device_id=place, device_id_type=MESH)
    load_t.wait()
    unit_rows(xt, wide, tl, tu, gt.at[plane])
    load_i.wait()
    unit_rows(xi, wide, il, iu, gi.at[me_i])
    r = lax.broadcasted_iota(jnp.int32, (24 * n_i, 1), 0)
    c = lax.broadcasted_iota(jnp.int32, (1, 24 * n_t), 1)
    g, r = member_row(r, n_i)
    h, c = member_row(c, n_t)
    row_ids = ((g % n_row) * (2 * n_t) + plane * 2 + g // n_row) * rows + r
    col_ids = ((h * 2 + core) * n_row + row) * rows + c
    label = jnp.where(row_ids == col_ids, F32(1.0), F32(-1.0))
    label_ref[...] = label
    temperature = jnp.exp(jnp.full((1, 1), scale_ref[...], F32))
    pl.semaphore_wait(barrier, n_row + n_t - 1)

    sent = []

    def push(src, dst, recv, place):
        copy = pltpu.make_async_remote_copy(
            src_ref=src, dst_ref=dst, send_sem=send_sem.at[len(sent)], recv_sem=recv,
            device_id=place, device_id_type=MESH)
        copy.start()
        sent.append(copy)

    def arrived(dst, recv):
        pltpu.make_async_remote_copy(
            src_ref=dst, dst_ref=dst, send_sem=send_sem.at[0], recv_sem=recv,
            device_id=sibling, device_id_type=MESH).wait_recv()

    for h in planes:
        push(gt.at[plane], gt.at[plane], ct.at[plane], at_plane(h))
    for r in other_rows:
        push(gi.at[me_i], gi.at[me_i], ci.at[me_i], at_row(r))
    push(gi.at[me_i], gi.at[me_i], ci.at[me_i], sibling)
    for r in other_rows:
        g = core * n_row + r
        arrived(gi.at[g], ci.at[g])
        push(gi.at[g], gi.at[g], ci.at[g], sibling)
    for r in [row] + other_rows:
        g = other_core * n_row + r
        arrived(gi.at[g], ci.at[g])
    images = all_rows(gi, width)
    for h in planes[::-1]:
        arrived(gt.at[h], ct.at[h])
    texts = all_rows(gt, width)
    scores = lax.dot_general(images, texts, (((1,), (1,)), ((), ())), preferred_element_type=F32)
    label = label_ref[...]
    margin = label * (temperature * scores + bias_ref[...])
    weights = -label * jax.nn.sigmoid(-margin)
    wt[...] = weights.T.astype(BF16)
    wh[...] = weights[:16 * n_i].astype(BF16)
    wl[...] = weights[16 * n_i:].astype(BF16)

    to_blocks(jnp.dot(wt[...], images, preferred_element_type=F32), pt)
    for h in planes:
        push(pt.at[h], rt.at[plane], ct2.at[plane], at_plane(h))

    def half(c):
        head = wh[pl.ds(pl.multiple_of(c * (16 * n_row), 16), 16 * n_row)]
        tail = wl[pl.ds(pl.multiple_of(c * (8 * n_row), 16), 8 * n_row)]
        return jnp.dot(jnp.concatenate([head, tail], axis=0), texts, preferred_element_type=F32)

    to_blocks(half(other_core), ps)
    push(ps, rs, pair_sem.at[0], sibling)
    to_blocks(half(core), po)
    arrived(rs, pair_sem.at[0])
    for r in other_rows:
        pi[r] = (po[r] + rs[r].astype(F32)).astype(BF16)
        push(pi.at[r], ri.at[row], ci2.at[row], at_row(r))

    def rows_of(total):
        return temperature * jnp.concatenate([total[:, :width], unpack_tail(total[:, width:], width)], axis=0)

    acc[...] = po[row] + rs[row].astype(F32)
    for r in other_rows:
        arrived(ri.at[r], ci2.at[r])
        acc[...] += ri[r].astype(F32)
    gimg_ref[...] = norm_back(iu[...], il[:, :1], rows_of(acc[...]))[:rows]
    acc[...] = pt[plane].astype(F32)
    for h in planes[::-1]:
        arrived(rt.at[h], ct2.at[h])
        acc[...] += rt[h].astype(F32)
    gtxt_ref[...] = norm_back(tu[...], tl[:, :1], rows_of(acc[...]))[:rows]
    for copy in sent:
        copy.wait_send()


def hand_over(gimg_ref, gtxt_ref, images_ref, texts_ref):
    images_ref[...] = gimg_ref[...]
    texts_ref[...] = gtxt_ref[...]


def on_device(n_row, n_col, images, texts, logarithmic_scale, similarity_bias):
    rows, width = images.shape
    pad = 24
    packed = width + -(-width // 256) * 128
    assert 16 < rows <= pad and n_col % 2 == 0 and n_row % 2 == 0
    n_i, n_t = 2 * n_row, n_col // 2
    vmem = pl.BlockSpec(memory_space=pltpu.VMEM)
    hbm = pl.BlockSpec(memory_space=pltpu.HBM)
    smem = pl.BlockSpec(memory_space=pltpu.SMEM)
    out = jax.ShapeDtypeStruct((rows, width), F32)
    dma = pltpu.SemaphoreType.DMA

    def blocks(n, kind=BF16):
        return pltpu.VMEM((n, 16, packed), kind)

    grads = pl.pallas_call(
        functools.partial(kernel, n_row, n_t),
        out_shape=(out, out),
        in_specs=[hbm, hbm, smem, smem],
        out_specs=(vmem, vmem),
        scratch_shapes=[
            pltpu.VMEM((rows, width), BF16),
            pltpu.VMEM((rows, width), BF16),
            pltpu.VMEM((pad, width), F32),
            pltpu.VMEM((pad, width), F32),
            pltpu.VMEM((pad, width), F32),
            pltpu.VMEM((pad, 128), F32),
            pltpu.VMEM((pad, 128), F32),
            blocks(n_i),
            blocks(n_t),
            pltpu.VMEM((n_i * pad, n_t * pad), F32),
            pltpu.VMEM((n_t * pad, n_i * pad), BF16),
            pltpu.VMEM((n_i * 16, n_t * pad), BF16),
            pltpu.VMEM((n_i * 8, n_t * pad), BF16),
            blocks(n_t),
            blocks(n_row),
            blocks(n_row, F32),
            blocks(n_row),
            pltpu.VMEM((16, packed), F32),
            blocks(n_t),
            blocks(n_row),
            blocks(n_row),
            dma((2,)), dma((3 * n_row + 2 * n_t + 2,)),
            dma((n_i,)), dma((n_t,)), dma((n_t,)), dma((n_row,)), dma((1,)),
        ],
        compiler_params=pltpu.CompilerParams(
            collective_id=0, has_side_effects=True),
    )(images, texts, logarithmic_scale, similarity_bias)
    return pl.pallas_call(
        hand_over, out_shape=(out, out), in_specs=[vmem, vmem], out_specs=(vmem, vmem))(*grads)


def solution(mesh):
    return jax.shard_map(
        functools.partial(on_device, mesh.shape["row"], mesh.shape["col"]),
        mesh=mesh,
        in_specs=(P(("row", "col"), None), P(("col", "row"), None), P(), P()),
        out_specs=(P(("row", "col"), None), P(("col", "row"), None)),
        check_vma=False,
    )
```

time: 25.2 us -> 22.8 us (0.905)
  local copies, waits for them, and re-layouts: 2.23 us -> 0 us
    unnamed x4 -> x0, local copies, waits for them, and re-layouts: 2.23 us -> none
    pallas_call x1, Pallas kernels: 20.8 us -> 19 us  [on_device(): pl.pallas_call(functools.partial(kernel, n_row, n_t), out_shape=(out, out...]
    pallas_call x0 -> x1, Pallas kernels: none -> 1.64 us  [on_device(): pl.pallas_call(hand_over, out_shape=(out, out), in_specs=[vmem, vmem], ou...]
where the time goes in v5:
time: 22.8 us; the launch traced here: 22.5 us
  Pallas kernels  20.6 us (90%)
  between operations  1.93 us (8%)
    pallas_call x1, Pallas kernels, on_device(): pl.pallas_call(functools.partial(kernel, n_row, n_t), out_shape=(out, out...  19 us
    pallas_call x1, Pallas kernels, on_device(): pl.pallas_call(hand_over, out_shape=(out, out), in_specs=[vmem, vmem], ou...  1.64 us

profile of v5, /device:TPU:0, one launch (start us, length us, event | category | flops | bytes accessed | tf_op | source)
XLA Modules:
  0.0 22.5 jit_solution(8792626837009012621)
XLA Ops:
  1.9 19.0 %shard_map.59 = (f32[22,1152]{1,0:T(8,128)}, f32[22,1152]{1,0:T(8,128)}) custom-call(bf16[22,1152]{1,0:T(8,128)(2,1)} %img_ref.1, bf16[22,1152]{1,0:T(8,128)(2,1)} %txt_ref.1, f32[]{:T(128)S(6)} %copy.6.scale_ref, f32[]{:T(128)S(6)} %copy.7.bias_ref), custom_call_target="tpu_custom_call" | custom-call | tf_op jit(solution)/shard_map/pallas_call | solution.py:206
  20.9 1.6 %shard_map.60 = (f32[22,1152]{1,0:T(8,128)}, f32[22,1152]{1,0:T(8,128)}) custom-call(f32[22,1152]{1,0:T(8,128)} %get-tuple-element.4.gimg_ref, f32[22,1152]{1,0:T(8,128)} %get-tuple-element.5.gtxt_ref), custom_call_target="tpu_custom_call" | custom-call | tf_op jit(solution)/shard_map/pallas_call | solution.py:239

commit v6 on v5

--- a/solution.py
+++ b/solution.py
@@ -65,7 +65,7 @@
 
 
 def kernel(n_row, n_t, img_ref, txt_ref, scale_ref, bias_ref, gimg_ref, gtxt_ref,
-           xi, xt, wide, iu, tu, il, tl, gi, gt, label_ref, wt, wh, wl, pt, ps, po, pi, acc, rt, rs, ri,
+           xi, xt, wide, iu, tu, il, tl, gi, gt, label_ref, im, tx, wt, wh, wl, pt, ps, po, pi, acc, rt, rs, ri,
            in_sem, send_sem, ci, ct, ct2, ci2, pair_sem):
     rows, width = img_ref.shape
     load_t = pltpu.make_async_copy(txt_ref, xt, in_sem.at[0])
@@ -100,14 +100,14 @@
     unit_rows(xt, wide, tl, tu, gt.at[plane])
     load_i.wait()
     unit_rows(xi, wide, il, iu, gi.at[me_i])
-    r = lax.broadcasted_iota(jnp.int32, (24 * n_i, 1), 0)
-    c = lax.broadcasted_iota(jnp.int32, (1, 24 * n_t), 1)
-    g, r = member_row(r, n_i)
-    h, c = member_row(c, n_t)
+    h_n = n_t // 2
+    slab = 24 * h_n
+    g, r = member_row(lax.broadcasted_iota(jnp.int32, (1, 24 * n_i), 1), n_i)
     row_ids = ((g % n_row) * (2 * n_t) + plane * 2 + g // n_row) * rows + r
-    col_ids = ((h * 2 + core) * n_row + row) * rows + c
-    label = jnp.where(row_ids == col_ids, F32(1.0), F32(-1.0))
-    label_ref[...] = label
+    h, c = member_row(lax.broadcasted_iota(jnp.int32, (slab, 1), 0), h_n)
+    for q in range(2):
+        col_ids = (((h + q * h_n) * 2 + core) * n_row + row) * rows + c
+        label_ref[q * slab:(q + 1) * slab] = jnp.where(row_ids == col_ids, F32(1.0), F32(-1.0))
     temperature = jnp.exp(jnp.full((1, 1), scale_ref[...], F32))
     pl.semaphore_wait(barrier, n_row + n_t - 1)
 
@@ -118,7 +118,7 @@
             src_ref=src, dst_ref=dst, send_sem=send_sem.at[len(sent)], recv_sem=recv,
             device_id=place, device_id_type=MESH)
         copy.start()
-        sent.append(copy)
+        sent.append((copy, None))
 
     def arrived(dst, recv):
         pltpu.make_async_remote_copy(
@@ -137,26 +137,46 @@
     for r in [row] + other_rows:
         g = other_core * n_row + r
         arrived(gi.at[g], ci.at[g])
-    images = all_rows(gi, width)
-    for h in planes[::-1]:
-        arrived(gt.at[h], ct.at[h])
-    texts = all_rows(gt, width)
-    scores = lax.dot_general(images, texts, (((1,), (1,)), ((), ())), preferred_element_type=F32)
-    label = label_ref[...]
-    margin = label * (temperature * scores + bias_ref[...])
-    weights = -label * jax.nn.sigmoid(-margin)
-    wt[...] = weights.T.astype(BF16)
-    wh[...] = weights[:16 * n_i].astype(BF16)
-    wl[...] = weights[16 * n_i:].astype(BF16)
-
-    to_blocks(jnp.dot(wt[...], images, preferred_element_type=F32), pt)
-    for h in planes:
-        push(pt.at[h], rt.at[plane], ct2.at[plane], at_plane(h))
+    im[...] = all_rows(gi[...], width)
+
+    mine = plane // h_n
+    first = jnp.where(from_end < (h_n + 1) // 2, 1 - mine, mine)
+    for q in (first, 1 - first):
+        for j in range(h_n):
+            h = q * h_n + j
+
+            @pl.when(h != plane)
+            def _():
+                arrived(gt.at[h], ct.at[h])
+
+        at = pl.ds(pl.multiple_of(q * slab, 16), slab)
+        tx[at] = all_rows(gt[pl.ds(q * h_n, h_n)], width)
+        scores = lax.dot_general(tx[at], im[...], (((1,), (1,)), ((), ())), preferred_element_type=F32)
+        label = label_ref[at]
+        margin = label * (temperature * scores + bias_ref[...])
+        wt[at] = (-label * jax.nn.sigmoid(-margin)).astype(BF16)
+        to_blocks(jnp.dot(wt[at], im[...], preferred_element_type=F32), pt.at[pl.ds(q * h_n, h_n)])
+        for j in range(h_n):
+            h = q * h_n + j
+            slot = send_sem.at[len(sent)]
+            copy = pltpu.make_async_remote_copy(
+                src_ref=pt.at[h], dst_ref=rt.at[plane], send_sem=slot, recv_sem=ct2.at[plane],
+                device_id=at_plane(h), device_id_type=MESH)
+
+            @pl.when(h != plane)
+            def _():
+                copy.start()
+
+            sent.append((copy, h != plane))
+
+    w = wt[...].astype(F32).T.astype(BF16)
+    wh[...] = w[:16 * n_i]
+    wl[...] = w[16 * n_i:]
 
     def half(c):
         head = wh[pl.ds(pl.multiple_of(c * (16 * n_row), 16), 16 * n_row)]
         tail = wl[pl.ds(pl.multiple_of(c * (8 * n_row), 16), 8 * n_row)]
-        return jnp.dot(jnp.concatenate([head, tail], axis=0), texts, preferred_element_type=F32)
+        return jnp.dot(jnp.concatenate([head, tail], axis=0), tx[...], preferred_element_type=F32)
 
     to_blocks(half(other_core), ps)
     push(ps, rs, pair_sem.at[0], sibling)
@@ -169,18 +189,21 @@
     def rows_of(total):
         return temperature * jnp.concatenate([total[:, :width], unpack_tail(total[:, width:], width)], axis=0)
 
-    acc[...] = po[row] + rs[row].astype(F32)
-    for r in other_rows:
-        arrived(ri.at[r], ci2.at[r])
-        acc[...] += ri[r].astype(F32)
-    gimg_ref[...] = norm_back(iu[...], il[:, :1], rows_of(acc[...]))[:rows]
     acc[...] = pt[plane].astype(F32)
     for h in planes[::-1]:
         arrived(rt.at[h], ct2.at[h])
         acc[...] += rt[h].astype(F32)
     gtxt_ref[...] = norm_back(tu[...], tl[:, :1], rows_of(acc[...]))[:rows]
-    for copy in sent:
-        copy.wait_send()
+    acc[...] = po[row] + rs[row].astype(F32)
+    for r in other_rows:
+        arrived(ri.at[r], ci2.at[r])
+        acc[...] += ri[r].astype(F32)
+    gimg_ref[...] = norm_back(iu[...], il[:, :1], rows_of(acc[...]))[:rows]
+    for copy, condition in sent:
+        if condition is None:
+            copy.wait_send()
+        else:
+            pl.when(condition)(copy.wait_send)
 
 
 def hand_over(gimg_ref, gtxt_ref, images_ref, texts_ref):
@@ -192,7 +215,7 @@
     rows, width = images.shape
     pad = 24
     packed = width + -(-width // 256) * 128
-    assert 16 < rows <= pad and n_col % 2 == 0 and n_row % 2 == 0
+    assert 16 < rows <= pad and n_col % 8 == 0 and n_row % 2 == 0
     n_i, n_t = 2 * n_row, n_col // 2
     vmem = pl.BlockSpec(memory_space=pltpu.VMEM)
     hbm = pl.BlockSpec(memory_space=pltpu.HBM)
@@ -218,7 +241,9 @@
             pltpu.VMEM((pad, 128), F32),
             blocks(n_i),
             blocks(n_t),
-            pltpu.VMEM((n_i * pad, n_t * pad), F32),
+            pltpu.VMEM((n_t * pad, n_i * pad), F32),
+            pltpu.VMEM((n_i * pad, width), BF16),
+            pltpu.VMEM((n_t * pad, width), BF16),
             pltpu.VMEM((n_t * pad, n_i * pad), BF16),
             pltpu.VMEM((n_i * 16, n_t * pad), BF16),
             pltpu.VMEM((n_i * 8, n_t * pad), BF16),
@@ -230,7 +255,7 @@
             blocks(n_t),
             blocks(n_row),
             blocks(n_row),
-            dma((2,)), dma((3 * n_row + 2 * n_t + 2,)),
+            dma((2,)), dma((3 * n_row + 2 * n_t + 4,)),
             dma((n_i,)), dma((n_t,)), dma((n_t,)), dma((n_row,)), dma((1,)),
         ],
         compiler_params=pltpu.CompilerParams(

time: 22.8 us -> 23.3 us (1.022)
  Pallas kernels: 20.6 us -> 21.2 us
    pallas_call x1, Pallas kernels: 19 us -> 19.5 us  [on_device(): pl.pallas_call(functools.partial(kernel, n_row, n_t), out_shape=(out, out...]
where the time goes in v6:
time: 23.3 us; the launch traced here: 23.1 us
  Pallas kernels  21.2 us (91%)
  between operations  1.93 us (8%)
    pallas_call x1, Pallas kernels, on_device(): pl.pallas_call(functools.partial(kernel, n_row, n_t), out_shape=(out, out...  19.5 us
    pallas_call x1, Pallas kernels, on_device(): pl.pallas_call(hand_over, out_shape=(out, out), in_specs=[vmem, vmem], ou...  1.64 us

profile of v6, /device:TPU:0, one launch (start us, length us, event | category | flops | bytes accessed | tf_op | source)
XLA Modules:
  0.0 23.1 jit_solution(5326918544698421633)
XLA Ops:
  1.9 19.5 %shard_map.59 = (f32[22,1152]{1,0:T(8,128)}, f32[22,1152]{1,0:T(8,128)}) custom-call(bf16[22,1152]{1,0:T(8,128)(2,1)} %img_ref.1, bf16[22,1152]{1,0:T(8,128)(2,1)} %txt_ref.1, f32[]{:T(128)S(6)} %copy.6.scale_ref, f32[]{:T(128)S(6)} %copy.7.bias_ref), custom_call_target="tpu_custom_call" | custom-call | tf_op jit(solution)/shard_map/pallas_call | solution.py:229
  21.4 1.6 %shard_map.60 = (f32[22,1152]{1,0:T(8,128)}, f32[22,1152]{1,0:T(8,128)}) custom-call(f32[22,1152]{1,0:T(8,128)} %get-tuple-element.4.gimg_ref, f32[22,1152]{1,0:T(8,128)} %get-tuple-element.5.gtxt_ref), custom_call_target="tpu_custom_call" | custom-call | tf_op jit(solution)/shard_map/pallas_call | solution.py:264

commit v7 on v5

--- a/solution.py
+++ b/solution.py
@@ -66,7 +66,7 @@
 
 def kernel(n_row, n_t, img_ref, txt_ref, scale_ref, bias_ref, gimg_ref, gtxt_ref,
            xi, xt, wide, iu, tu, il, tl, gi, gt, label_ref, wt, wh, wl, pt, ps, po, pi, acc, rt, rs, ri,
-           in_sem, send_sem, ci, ct, ct2, ci2, pair_sem):
+           in_sem, line_sem, send_sem, ci, ct, ct2, ci2, pair_sem):
     rows, width = img_ref.shape
     load_t = pltpu.make_async_copy(txt_ref, xt, in_sem.at[0])
     load_i = pltpu.make_async_copy(img_ref, xi, in_sem.at[1])
@@ -83,6 +83,10 @@
     for t in range(n_t - 1, 0, -1):
         t = jnp.where(t > from_end, t, t - 1)
         planes.append(jnp.where(low, t, n_t - 1 - t))
+
+    line = n_t == 4
+    is_end, is_relay = from_end == 0, from_end == 1
+    far_end, near_end = jnp.where(low, 3, 0), jnp.where(low, 0, 3)
 
     def at_row(r):
         return (r, col)
@@ -125,21 +129,49 @@
             src_ref=dst, dst_ref=dst, send_sem=send_sem.at[0], recv_sem=recv,
             device_id=sibling, device_id_type=MESH).wait_recv()
 
-    for h in planes:
-        push(gt.at[plane], gt.at[plane], ct.at[plane], at_plane(h))
+    def text_copy(block, h, slot):
+        return pltpu.make_async_remote_copy(
+            src_ref=gt.at[block], dst_ref=gt.at[block], send_sem=line_sem.at[slot],
+            recv_sem=ct.at[block], device_id=at_plane(h), device_id_type=MESH)
+
+    if line:
+        across, inner, near = planes[0], planes[1], planes[2]
+        text_copy(plane, inner, 1).start()
+
+        @pl.when(is_relay)
+        def _():
+            text_copy(plane, across, 0).start()
+
+        text_copy(plane, near, 2).start()
+    else:
+        for h in planes:
+            push(gt.at[plane], gt.at[plane], ct.at[plane], at_plane(h))
     for r in other_rows:
         push(gi.at[me_i], gi.at[me_i], ci.at[me_i], at_row(r))
     push(gi.at[me_i], gi.at[me_i], ci.at[me_i], sibling)
-    for r in other_rows:
+    for k, r in enumerate(other_rows):
         g = core * n_row + r
         arrived(gi.at[g], ci.at[g])
         push(gi.at[g], gi.at[g], ci.at[g], sibling)
+        if line and k == 0:
+            @pl.when(is_relay)
+            def _():
+                arrived(gt.at[far_end], ct.at[far_end])
+                text_copy(far_end, near_end, 3).start()
     for r in [row] + other_rows:
         g = other_core * n_row + r
         arrived(gi.at[g], ci.at[g])
     images = all_rows(gi, width)
-    for h in planes[::-1]:
-        arrived(gt.at[h], ct.at[h])
+    if line:
+        arrived(gt.at[near], ct.at[near])
+        arrived(gt.at[inner], ct.at[inner])
+
+        @pl.when(is_end)
+        def _():
+            arrived(gt.at[far_end], ct.at[far_end])
+    else:
+        for h in planes[::-1]:
+            arrived(gt.at[h], ct.at[h])
     texts = all_rows(gt, width)
     scores = lax.dot_general(images, texts, (((1,), (1,)), ((), ())), preferred_element_type=F32)
     label = label_ref[...]
@@ -181,6 +213,14 @@
     gtxt_ref[...] = norm_back(tu[...], tl[:, :1], rows_of(acc[...]))[:rows]
     for copy in sent:
         copy.wait_send()
+    if line:
+        text_copy(plane, inner, 1).wait_send()
+        text_copy(plane, near, 2).wait_send()
+
+        @pl.when(is_relay)
+        def _():
+            text_copy(plane, across, 0).wait_send()
+            text_copy(far_end, near_end, 3).wait_send()
 
 
 def hand_over(gimg_ref, gtxt_ref, images_ref, texts_ref):
@@ -230,7 +270,7 @@
             blocks(n_t),
             blocks(n_row),
             blocks(n_row),
-            dma((2,)), dma((3 * n_row + 2 * n_t + 2,)),
+            dma((2,)), dma((4,)), dma((3 * n_row + 2 * n_t + 2,)),
             dma((n_i,)), dma((n_t,)), dma((n_t,)), dma((n_row,)), dma((1,)),
         ],
         compiler_params=pltpu.CompilerParams(

time: 22.8 us -> 23.8 us (1.044)
  Pallas kernels: 20.6 us -> 21.6 us
    pallas_call x1, Pallas kernels: 19 us -> 20 us  [on_device(): pl.pallas_call(functools.partial(kernel, n_row, n_t), out_shape=(out, out...]
where the time goes in v7:
time: 23.8 us; the launch traced here: 23.6 us
  Pallas kernels  21.6 us (91%)
  between operations  1.93 us (8%)
    pallas_call x1, Pallas kernels, on_device(): pl.pallas_call(functools.partial(kernel, n_row, n_t), out_shape=(out, out...  20 us
    pallas_call x1, Pallas kernels, on_device(): pl.pallas_call(hand_over, out_shape=(out, out), in_specs=[vmem, vmem], ou...  1.64 us

profile of v7, /device:TPU:0, one launch (start us, length us, event | category | flops | bytes accessed | tf_op | source)
XLA Modules:
  0.0 23.6 jit_solution(6682467116788422728)
XLA Ops:
  1.9 20.0 %shard_map.59 = (f32[22,1152]{1,0:T(8,128)}, f32[22,1152]{1,0:T(8,128)}) custom-call(bf16[22,1152]{1,0:T(8,128)(2,1)} %img_ref.1, bf16[22,1152]{1,0:T(8,128)(2,1)} %txt_ref.1, f32[]{:T(128)S(6)} %copy.6.scale_ref, f32[]{:T(128)S(6)} %copy.7.bias_ref), custom_call_target="tpu_custom_call" | custom-call | tf_op jit(solution)/shard_map/pallas_call | solution.py:246
  21.9 1.6 %shard_map.60 = (f32[22,1152]{1,0:T(8,128)}, f32[22,1152]{1,0:T(8,128)}) custom-call(f32[22,1152]{1,0:T(8,128)} %get-tuple-element.4.gimg_ref, f32[22,1152]{1,0:T(8,128)} %get-tuple-element.5.gtxt_ref), custom_call_target="tpu_custom_call" | custom-call | tf_op jit(solution)/shard_map/pallas_call | solution.py:279

commit v8 on v5

--- a/solution.py
+++ b/solution.py
@@ -65,8 +65,8 @@
 
 
 def kernel(n_row, n_t, img_ref, txt_ref, scale_ref, bias_ref, gimg_ref, gtxt_ref,
-           xi, xt, wide, iu, tu, il, tl, gi, gt, label_ref, wt, wh, wl, pt, ps, po, pi, acc, rt, rs, ri,
-           in_sem, send_sem, ci, ct, ct2, ci2, pair_sem):
+           oi, ot, xi, xt, wide, iu, tu, il, tl, gi, gt, label_ref, im, imt, wh, wl, pt, ps, po, pi, acc, rt, rs, ri,
+           in_sem, out_sem, send_sem, ci, ct, ct2, ci2, pair_sem):
     rows, width = img_ref.shape
     load_t = pltpu.make_async_copy(txt_ref, xt, in_sem.at[0])
     load_i = pltpu.make_async_copy(img_ref, xi, in_sem.at[1])
@@ -100,8 +100,8 @@
     unit_rows(xt, wide, tl, tu, gt.at[plane])
     load_i.wait()
     unit_rows(xi, wide, il, iu, gi.at[me_i])
-    r = lax.broadcasted_iota(jnp.int32, (24 * n_i, 1), 0)
-    c = lax.broadcasted_iota(jnp.int32, (1, 24 * n_t), 1)
+    r = lax.broadcasted_iota(jnp.int32, (1, 24 * n_i), 1)
+    c = lax.broadcasted_iota(jnp.int32, (24 * n_t, 1), 0)
     g, r = member_row(r, n_i)
     h, c = member_row(c, n_t)
     row_ids = ((g % n_row) * (2 * n_t) + plane * 2 + g // n_row) * rows + r
@@ -137,21 +137,22 @@
     for r in [row] + other_rows:
         g = other_core * n_row + r
         arrived(gi.at[g], ci.at[g])
-    images = all_rows(gi, width)
+    im[...] = all_rows(gi, width)
+    imt[...] = im[...].T
     for h in planes[::-1]:
         arrived(gt.at[h], ct.at[h])
     texts = all_rows(gt, width)
-    scores = lax.dot_general(images, texts, (((1,), (1,)), ((), ())), preferred_element_type=F32)
+    scores = jnp.dot(texts, imt[...], preferred_element_type=F32)
     label = label_ref[...]
     margin = label * (temperature * scores + bias_ref[...])
     weights = -label * jax.nn.sigmoid(-margin)
-    wt[...] = weights.T.astype(BF16)
-    wh[...] = weights[:16 * n_i].astype(BF16)
-    wl[...] = weights[16 * n_i:].astype(BF16)
-
-    to_blocks(jnp.dot(wt[...], images, preferred_element_type=F32), pt)
+    to_blocks(jnp.dot(weights.astype(BF16), im[...], preferred_element_type=F32), pt)
     for h in planes:
         push(pt.at[h], rt.at[plane], ct2.at[plane], at_plane(h))
+
+    weights = weights.T.astype(BF16)
+    wh[...] = weights[:16 * n_i]
+    wl[...] = weights[16 * n_i:]
 
     def half(c):
         head = wh[pl.ds(pl.multiple_of(c * (16 * n_row), 16), 16 * n_row)]
@@ -173,14 +174,20 @@
     for r in other_rows:
         arrived(ri.at[r], ci2.at[r])
         acc[...] += ri[r].astype(F32)
-    gimg_ref[...] = norm_back(iu[...], il[:, :1], rows_of(acc[...]))[:rows]
+    oi[...] = norm_back(iu[...], il[:, :1], rows_of(acc[...]))[:rows]
+    out_i = pltpu.make_async_copy(oi, gimg_ref, out_sem.at[0])
+    out_i.start()
     acc[...] = pt[plane].astype(F32)
     for h in planes[::-1]:
         arrived(rt.at[h], ct2.at[h])
         acc[...] += rt[h].astype(F32)
-    gtxt_ref[...] = norm_back(tu[...], tl[:, :1], rows_of(acc[...]))[:rows]
+    ot[...] = norm_back(tu[...], tl[:, :1], rows_of(acc[...]))[:rows]
+    out_t = pltpu.make_async_copy(ot, gtxt_ref, out_sem.at[1])
+    out_t.start()
     for copy in sent:
         copy.wait_send()
+    out_i.wait()
+    out_t.wait()
 
 
 def hand_over(gimg_ref, gtxt_ref, images_ref, texts_ref):
@@ -207,8 +214,10 @@
         functools.partial(kernel, n_row, n_t),
         out_shape=(out, out),
         in_specs=[hbm, hbm, smem, smem],
-        out_specs=(vmem, vmem),
+        out_specs=(hbm, hbm),
         scratch_shapes=[
+            pltpu.VMEM((rows, width), F32),
+            pltpu.VMEM((rows, width), F32),
             pltpu.VMEM((rows, width), BF16),
             pltpu.VMEM((rows, width), BF16),
             pltpu.VMEM((pad, width), F32),
@@ -218,8 +227,9 @@
             pltpu.VMEM((pad, 128), F32),
             blocks(n_i),
             blocks(n_t),
-            pltpu.VMEM((n_i * pad, n_t * pad), F32),
-            pltpu.VMEM((n_t * pad, n_i * pad), BF16),
+            pltpu.VMEM((n_t * pad, n_i * pad), F32),
+            pltpu.VMEM((n_i * pad, width), BF16),
+            pltpu.VMEM((width, n_i * pad), BF16),
             pltpu.VMEM((n_i * 16, n_t * pad), BF16),
             pltpu.VMEM((n_i * 8, n_t * pad), BF16),
             blocks(n_t),
@@ -230,7 +240,7 @@
             blocks(n_t),
             blocks(n_row),
             blocks(n_row),
-            dma((2,)), dma((3 * n_row + 2 * n_t + 2,)),
+            dma((2,)), dma((2,)), dma((3 * n_row + 2 * n_t + 2,)),
             dma((n_i,)), dma((n_t,)), dma((n_t,)), dma((n_row,)), dma((1,)),
         ],
         compiler_params=pltpu.CompilerParams(

time: 22.8 us -> 22.8 us (level)
  no operation moved by 1% of the time
where the time goes in v8:
time: 22.8 us; the launch traced here: 22.6 us
  Pallas kernels  20.6 us (90%)
  between operations  1.93 us (8%)
    pallas_call x1, Pallas kernels, on_device(): pl.pallas_call(functools.partial(kernel, n_row, n_t), out_shape=(out, out...  19 us
    pallas_call x1, Pallas kernels, on_device(): pl.pallas_call(hand_over, out_shape=(out, out), in_specs=[vmem, vmem], ou...  1.64 us

profile of v8, /device:TPU:0, one launch (start us, length us, event | category | flops | bytes accessed | tf_op | source)
XLA Modules:
  0.0 22.6 jit_solution(4941920967837355537)
XLA Ops:
  1.9 19.0 %shard_map.59 = (f32[22,1152]{1,0:T(8,128)}, f32[22,1152]{1,0:T(8,128)}) custom-call(bf16[22,1152]{1,0:T(8,128)(2,1)} %img_ref.1, bf16[22,1152]{1,0:T(8,128)(2,1)} %txt_ref.1, f32[]{:T(128)S(6)} %copy.6.scale_ref, f32[]{:T(128)S(6)} %copy.7.bias_ref), custom_call_target="tpu_custom_call" | custom-call | tf_op jit(solution)/shard_map/pallas_call | solution.py:213
  20.9 1.6 %shard_map.60 = (f32[22,1152]{1,0:T(8,128)}, f32[22,1152]{1,0:T(8,128)}) custom-call(f32[22,1152]{1,0:T(8,128)} %get-tuple-element.4.gimg_ref, f32[22,1152]{1,0:T(8,128)} %get-tuple-element.5.gtxt_ref), custom_call_target="tpu_custom_call" | custom-call | tf_op jit(solution)/shard_map/pallas_call | solution.py:249

commit v9 on v8

--- a/solution.py
+++ b/solution.py
@@ -65,13 +65,9 @@
 
 
 def kernel(n_row, n_t, img_ref, txt_ref, scale_ref, bias_ref, gimg_ref, gtxt_ref,
-           oi, ot, xi, xt, wide, iu, tu, il, tl, gi, gt, label_ref, im, imt, wh, wl, pt, ps, po, pi, acc, rt, rs, ri,
-           in_sem, out_sem, send_sem, ci, ct, ct2, ci2, pair_sem):
+           wide, iu, tu, il, tl, gi, gt, label_ref, im, imt, wh, wl, pt, ps, po, pi, acc, rt, rs, ri,
+           send_sem, ci, ct, ct2, ci2, pair_sem):
     rows, width = img_ref.shape
-    load_t = pltpu.make_async_copy(txt_ref, xt, in_sem.at[0])
-    load_i = pltpu.make_async_copy(img_ref, xi, in_sem.at[1])
-    load_t.start()
-    load_i.start()
     n_i = 2 * n_row
     row, col = lax.axis_index("row"), lax.axis_index("col")
     plane, core = col // 2, col % 2
@@ -96,10 +92,8 @@
     barrier = pltpu.get_barrier_semaphore()
     for place in [at_plane(h) for h in planes] + [at_row(r) for r in other_rows] + [sibling]:
         pl.semaphore_signal(barrier, inc=1, device_id=place, device_id_type=MESH)
-    load_t.wait()
-    unit_rows(xt, wide, tl, tu, gt.at[plane])
-    load_i.wait()
-    unit_rows(xi, wide, il, iu, gi.at[me_i])
+    unit_rows(txt_ref, wide, tl, tu, gt.at[plane])
+    unit_rows(img_ref, wide, il, iu, gi.at[me_i])
     r = lax.broadcasted_iota(jnp.int32, (1, 24 * n_i), 1)
     c = lax.broadcasted_iota(jnp.int32, (24 * n_t, 1), 0)
     g, r = member_row(r, n_i)
@@ -174,20 +168,14 @@
     for r in other_rows:
         arrived(ri.at[r], ci2.at[r])
         acc[...] += ri[r].astype(F32)
-    oi[...] = norm_back(iu[...], il[:, :1], rows_of(acc[...]))[:rows]
-    out_i = pltpu.make_async_copy(oi, gimg_ref, out_sem.at[0])
-    out_i.start()
+    gimg_ref[...] = norm_back(iu[...], il[:, :1], rows_of(acc[...]))[:rows]
     acc[...] = pt[plane].astype(F32)
     for h in planes[::-1]:
         arrived(rt.at[h], ct2.at[h])
         acc[...] += rt[h].astype(F32)
-    ot[...] = norm_back(tu[...], tl[:, :1], rows_of(acc[...]))[:rows]
-    out_t = pltpu.make_async_copy(ot, gtxt_ref, out_sem.at[1])
-    out_t.start()
+    gtxt_ref[...] = norm_back(tu[...], tl[:, :1], rows_of(acc[...]))[:rows]
     for copy in sent:
         copy.wait_send()
-    out_i.wait()
-    out_t.wait()
 
 
 def hand_over(gimg_ref, gtxt_ref, images_ref, texts_ref):
@@ -202,7 +190,6 @@
     assert 16 < rows <= pad and n_col % 2 == 0 and n_row % 2 == 0
     n_i, n_t = 2 * n_row, n_col // 2
     vmem = pl.BlockSpec(memory_space=pltpu.VMEM)
-    hbm = pl.BlockSpec(memory_space=pltpu.HBM)
     smem = pl.BlockSpec(memory_space=pltpu.SMEM)
     out = jax.ShapeDtypeStruct((rows, width), F32)
     dma = pltpu.SemaphoreType.DMA
@@ -213,13 +200,9 @@
     grads = pl.pallas_call(
         functools.partial(kernel, n_row, n_t),
         out_shape=(out, out),
-        in_specs=[hbm, hbm, smem, smem],
-        out_specs=(hbm, hbm),
+        in_specs=[vmem, vmem, smem, smem],
+        out_specs=(vmem, vmem),
         scratch_shapes=[
-            pltpu.VMEM((rows, width), F32),
-            pltpu.VMEM((rows, width), F32),
-            pltpu.VMEM((rows, width), BF16),
-            pltpu.VMEM((rows, width), BF16),
             pltpu.VMEM((pad, width), F32),
             pltpu.VMEM((pad, width), F32),
             pltpu.VMEM((pad, width), F32),
@@ -240,11 +223,12 @@
             blocks(n_t),
             blocks(n_row),
             blocks(n_row),
-            dma((2,)), dma((2,)), dma((3 * n_row + 2 * n_t + 2,)),
+            dma((3 * n_row + 2 * n_t + 2,)),
             dma((n_i,)), dma((n_t,)), dma((n_t,)), dma((n_row,)), dma((1,)),
         ],
         compiler_params=pltpu.CompilerParams(
-            collective_id=0, has_side_effects=True),
+            collective_id=0, has_side_effects=True,
+            vmem_limit_bytes=48 * 2**20),
     )(images, texts, logarithmic_scale, similarity_bias)
     return pl.pallas_call(
         hand_over, out_shape=(out, out), in_specs=[vmem, vmem], out_specs=(vmem, vmem))(*grads)

time: 22.8 us -> 25 us (1.096)
  local copies, waits for them, and re-layouts: 0 us -> 2.88 us
  Pallas kernels: 20.6 us -> 19.9 us
    unnamed x0 -> x8, local copies, waits for them, and re-layouts: none -> 2.88 us
    pallas_call x1, Pallas kernels: 19 us -> 18.3 us  [on_device(): pl.pallas_call(functools.partial(kernel, n_row, n_t), out_shape=(out, out...]
where the time goes in v9:
time: 25 us; the launch traced here: 24.7 us
  Pallas kernels  19.9 us (80%)
  local copies, waits for them, and re-layouts  2.88 us (12%)
  between operations  1.95 us (8%)
    pallas_call x1, Pallas kernels, on_device(): pl.pallas_call(functools.partial(kernel, n_row, n_t), out_shape=(out, out...  18.3 us
    unnamed x8, local copies, waits for them, and re-layouts  2.88 us
    pallas_call x1, Pallas kernels, on_device(): pl.pallas_call(hand_over, out_shape=(out, out), in_specs=[vmem, vmem], ou...  1.64 us

profile of v9, /device:TPU:0, one launch (start us, length us, event | category | flops | bytes accessed | tf_op | source)
XLA Modules:
  0.0 24.7 jit_solution(6167044098984503418)
XLA Ops:
  1.9 0.0 copy-start.2
  1.9 0.8 %copy-done.2 = bf16[22,1152]{1,0:T(8,128)(2,1)S(1)} copy-done((bf16[22,1152]{1,0:T(8,128)(2,1)S(1)}, bf16[22,1152]{1,0:T(8,128)(2,1)}, u32[]{:S(2)}) %copy-start.2) | copy-done | bytes 50712
  2.7 0.0 copy-start.3
  2.7 0.8 %copy-done.3 = bf16[22,1152]{1,0:T(8,128)(2,1)S(1)} copy-done((bf16[22,1152]{1,0:T(8,128)(2,1)S(1)}, bf16[22,1152]{1,0:T(8,128)(2,1)}, u32[]{:S(2)}) %copy-start.3) | copy-done | bytes 50712
  3.6 18.3 %shard_map.59 = (f32[22,1152]{1,0:T(8,128)S(1)}, f32[22,1152]{1,0:T(8,128)S(1)}) custom-call(bf16[22,1152]{1,0:T(8,128)(2,1)S(1)} %copy-done.2, bf16[22,1152]{1,0:T(8,128)(2,1)S(1)} %copy-done.3, f32[]{:T(128)S(6)} %copy.6.scale_ref, f32[]{:T(128)S(6)} %copy.7.bias_ref), custom_call_target="tpu_custom_call" | custom-call | tf_op jit(solution)/shard_map/pallas_call | solution.py:200
  21.8 0.0 copy-start
  21.8 0.6 %copy-done = f32[22,1152]{1,0:T(8,128)} copy-done((f32[22,1152]{1,0:T(8,128)}, f32[22,1152]{1,0:T(8,128)S(1)}, u32[]{:S(2)}) %copy-start) | copy-done | bytes 101400
  22.5 0.0 copy-start.1
  22.5 0.6 %copy-done.1 = f32[22,1152]{1,0:T(8,128)} copy-done((f32[22,1152]{1,0:T(8,128)}, f32[22,1152]{1,0:T(8,128)S(1)}, u32[]{:S(2)}) %copy-start.1) | copy-done | bytes 101400
  23.1 1.6 %shard_map.60 = (f32[22,1152]{1,0:T(8,128)}, f32[22,1152]{1,0:T(8,128)}) custom-call(f32[22,1152]{1,0:T(8,128)} %copy-done, f32[22,1152]{1,0:T(8,128)} %copy-done.1), custom_call_target="tpu_custom_call" | custom-call | tf_op jit(solution)/shard_map/pallas_call | solution.py:233
Async XLA Ops:
  1.9 0.8 %copy-start.2 = (bf16[22,1152]{1,0:T(8,128)(2,1)S(1)}, bf16[22,1152]{1,0:T(8,128)(2,1)}, u32[]{:S(2)}) copy-start(bf16[22,1152]{1,0:T(8,128)(2,1)} %img_ref.1) | copy-start | bytes 152068
  2.7 0.8 %copy-start.3 = (bf16[22,1152]{1,0:T(8,128)(2,1)S(1)}, bf16[22,1152]{1,0:T(8,128)(2,1)}, u32[]{:S(2)}) copy-start(bf16[22,1152]{1,0:T(8,128)(2,1)} %txt_ref.1) | copy-start | bytes 152068
  21.8 0.6 %copy-start = (f32[22,1152]{1,0:T(8,128)}, f32[22,1152]{1,0:T(8,128)S(1)}, u32[]{:S(2)}) copy-start(f32[22,1152]{1,0:T(8,128)S(1)} %get-tuple-element.4.gimg_ref) | copy-start | bytes 304132
  22.5 0.6 %copy-start.1 = (f32[22,1152]{1,0:T(8,128)}, f32[22,1152]{1,0:T(8,128)S(1)}, u32[]{:S(2)}) copy-start(f32[22,1152]{1,0:T(8,128)S(1)} %get-tuple-element.5.gtxt_ref) | copy-start | bytes 304132

commit v10 on v5

--- a/solution.py
+++ b/solution.py
@@ -145,13 +145,8 @@
     label = label_ref[...]
     margin = label * (temperature * scores + bias_ref[...])
     weights = -label * jax.nn.sigmoid(-margin)
-    wt[...] = weights.T.astype(BF16)
     wh[...] = weights[:16 * n_i].astype(BF16)
     wl[...] = weights[16 * n_i:].astype(BF16)
-
-    to_blocks(jnp.dot(wt[...], images, preferred_element_type=F32), pt)
-    for h in planes:
-        push(pt.at[h], rt.at[plane], ct2.at[plane], at_plane(h))
 
     def half(c):
         head = wh[pl.ds(pl.multiple_of(c * (16 * n_row), 16), 16 * n_row)]
@@ -160,6 +155,10 @@
 
     to_blocks(half(other_core), ps)
     push(ps, rs, pair_sem.at[0], sibling)
+    wt[...] = weights.T.astype(BF16)
+    to_blocks(jnp.dot(wt[...], images, preferred_element_type=F32), pt)
+    for h in planes:
+        push(pt.at[h], rt.at[plane], ct2.at[plane], at_plane(h))
     to_blocks(half(core), po)
     arrived(rs, pair_sem.at[0])
     for r in other_rows:

time: 22.8 us -> 22.6 us (level)
  no operation moved by 1% of the time
where the time goes in v10:
time: 22.6 us; the launch traced here: 22.4 us
  Pallas kernels  20.5 us (91%)
  between operations  1.93 us (9%)
    pallas_call x1, Pallas kernels, on_device(): pl.pallas_call(functools.partial(kernel, n_row, n_t), out_shape=(out, out...  18.8 us
    pallas_call x1, Pallas kernels, on_device(): pl.pallas_call(hand_over, out_shape=(out, out), in_specs=[vmem, vmem], ou...  1.64 us

profile of v10, /device:TPU:0, one launch (start us, length us, event | category | flops | bytes accessed | tf_op | source)
XLA Modules:
  0.0 22.4 jit_solution(9751976066434690930)
XLA Ops:
  1.9 18.8 %shard_map.59 = (f32[22,1152]{1,0:T(8,128)}, f32[22,1152]{1,0:T(8,128)}) custom-call(bf16[22,1152]{1,0:T(8,128)(2,1)} %img_ref.1, bf16[22,1152]{1,0:T(8,128)(2,1)} %txt_ref.1, f32[]{:T(128)S(6)} %copy.6.scale_ref, f32[]{:T(128)S(6)} %copy.7.bias_ref), custom_call_target="tpu_custom_call" | custom-call | tf_op jit(solution)/shard_map/pallas_call | solution.py:205
  20.7 1.6 %shard_map.60 = (f32[22,1152]{1,0:T(8,128)}, f32[22,1152]{1,0:T(8,128)}) custom-call(f32[22,1152]{1,0:T(8,128)} %get-tuple-element.4.gimg_ref, f32[22,1152]{1,0:T(8,128)} %get-tuple-element.5.gtxt_ref), custom_call_target="tpu_custom_call" | custom-call | tf_op jit(solution)/shard_map/pallas_call | solution.py:238
